TPU v7x, 128 devices: a whole 4x4x4 slice. The times are simulated.
128 devices in a mesh: dp: 2 (over core), sect: 16 (over y, x), head: 4 (over z).
Axes of the slice: x: 4, y: 4, z: 4, core: 2. Of those that a mesh axis runs over, the one named last changes fastest.
Arguments:
- activations: bfloat16 [2, 4096, 4096], P('dp', 'sect'), may hold values from -6 to 6
- modality: int32 [2, 4096], P('dp', 'sect'), may hold values from 0 to 1, as said below
- query_rows: bfloat16 [2, 4096, 2048], P('dp', 'sect', 'head')
- key_rows: bfloat16 [2, 4096, 2048], P('dp', 'sect', 'head')
- value_weight: bfloat16 [2, 4096, 2048], P(None, 'sect', 'head'), may hold values from -0.09375 to 0.09375
- context_grad: bfloat16 [2, 4096, 2048], P('dp', 'sect', 'head'), may hold values from -6 to 6
Outputs:
- context: bfloat16 [2, 4096, 2048], P('dp', 'sect', 'head')
- input_grad: bfloat16 [2, 4096, 4096], P('dp', 'sect', 'head')
- weight_grad: float32 [2, 4096, 2048], P(None, 'sect', 'head')
Inputs may be any that keep to these rules, and one draw needn't show every extreme that they name: `modality`: each sequence holds exactly one image span of 1024 positions (value 1) that starts at a multiple of 128; every other position is text (value 0).
All inputs are finite; a program needn't handle non-finite values.
Results may differ from a plain program's by a relative error of at most 0.015.
Values may be sent and summed in bfloat16 or wider, within the bound.
A program may use at most 128 MiB of HBM per device.

v0:
```python
import jax
import jax.numpy as jnp
from jax import lax
from jax.sharding import PartitionSpec as P

HD = 128
BLOCK = 128


def blend(rows_in, is_image, weights, form):
    text_part = jnp.einsum(form, rows_in, weights[0], preferred_element_type=jnp.float32)
    image_part = jnp.einsum(form, rows_in, weights[1], preferred_element_type=jnp.float32)
    return jnp.where(is_image, image_part, text_part)


def expand_kinds(kinds):
    return (jnp.repeat(kinds, BLOCK, axis=1) == 1)[:, :, None]


def shards(activations, modality, query_rows, key_rows, value_weight, context_grad):
    seq_count, row_count, feat_width = activations.shape
    inner_width = value_weight.shape[2]
    full_length = row_count * lax.axis_size("sect")
    head_count = inner_width // HD
    score_scale = HD ** (-0.5)
    own_kinds = modality.reshape(seq_count, row_count // BLOCK, BLOCK)[:, :, 0]
    own_image = (modality == 1)[:, :, None]
    all_kinds = lax.all_gather(own_kinds, "sect", axis=1, tiled=True)
    columns = lax.all_to_all(activations, "sect", split_axis=2, concat_axis=1, tiled=True)
    features = activations
    value_sum = blend(
        features, own_image, lax.all_gather(value_weight, "sect", axis=1, tiled=True), "btf,fc->btc"
    )
    value = value_sum.astype(jnp.bfloat16)
    keys_all, values_all = (
        lax.all_gather(key_rows, "sect", axis=1, tiled=True),
        lax.all_gather(value, "sect", axis=1, tiled=True),
    )
    query_heads = query_rows.reshape(seq_count, row_count, head_count, HD)
    key_heads = keys_all.reshape(seq_count, full_length, head_count, HD)
    value_heads = values_all.reshape(seq_count, full_length, head_count, HD)
    scores = (
        jnp.einsum("bqhd,bkhd->bhqk", query_heads, key_heads, preferred_element_type=jnp.float32)
        * score_scale
    )
    first_row = lax.axis_index("sect") * row_count
    allowed = (first_row + jnp.arange(row_count))[:, None] >= jnp.arange(full_length)[None, :]
    scores = jnp.where(allowed, scores, -1e30)
    highest = jnp.max(scores, axis=3, keepdims=True)
    powers = jnp.exp(scores - highest)
    probs = (powers / jnp.sum(powers, axis=3, keepdims=True)).astype(jnp.bfloat16)
    context = jnp.einsum("bhqk,bkhd->bqhd", probs, value_heads, preferred_element_type=jnp.float32)
    context = context.astype(jnp.bfloat16).reshape(seq_count, row_count, inner_width)
    grad_heads = context_grad.reshape(seq_count, row_count, head_count, HD)
    term = jnp.einsum("bhqk,bqhd->kbhd", probs, grad_heads, preferred_element_type=jnp.float32)
    value_grad = lax.psum_scatter(
        term.reshape(row_count * lax.axis_size("sect"), seq_count, inner_width),
        "sect",
        scatter_dimension=0,
        tiled=True,
    )
    value_grad = value_grad.transpose(1, 0, 2).astype(jnp.bfloat16)
    zero_grad = jnp.zeros_like(value_grad[:1, :1, :1])
    shard_piece = lax.all_gather(value_grad, "sect", axis=1, tiled=True)
    features = columns
    is_image = expand_kinds(all_kinds)
    text_grads = jnp.where(is_image, zero_grad, shard_piece)
    image_grads = jnp.where(is_image, shard_piece, zero_grad)
    text_update = jnp.einsum(
        "btf,btc->fc", features, text_grads, preferred_element_type=jnp.float32
    )
    image_update = jnp.einsum(
        "btf,btc->fc", features, image_grads, preferred_element_type=jnp.float32
    )
    weight_sum = jnp.stack([text_update, image_update])
    back_rows = blend(shard_piece, is_image, value_weight, "btc,fc->btf")
    input_part = back_rows
    weight_local, input_part = (weight_sum, input_part)
    weight_grad = lax.psum(weight_local.astype(jnp.bfloat16), "dp").astype(jnp.float32)
    regrouped = lax.all_to_all(
        input_part.astype(jnp.bfloat16), "sect", split_axis=1, concat_axis=2, tiled=True
    ).astype(input_part.dtype)
    input_grad = lax.psum_scatter(
        regrouped.astype(jnp.bfloat16), "head", scatter_dimension=2, tiled=True
    )
    return (context, input_grad, weight_grad)


def solution(mesh):
    return jax.shard_map(
        shards,
        mesh=mesh,
        in_specs=(
            P("dp", "sect", None),
            P("dp", "sect"),
            P("dp", "sect", "head"),
            P("dp", "sect", "head"),
            P(None, "sect", "head"),
            P("dp", "sect", "head"),
        ),
        out_specs=(P("dp", "sect", "head"), P("dp", "sect", "head"), P(None, "sect", "head")),
        check_vma=False,
    )
```

profile of v0, /device:TPU:2, one launch (start us, length us, event | category | flops | bytes accessed | tf_op | source)
XLA Modules:
  0.0 492.1 jit_solution(12321452685089432759)
XLA Ops:
  7.2 1.8 copy.59
  9.1 1.0 reshape.132
  10.1 1.1 copy.74
  11.2 0.7 iota_compare_fusion
  11.9 58.3 %all-gather.10.cloned.1.call-done = bf16[1,4096,512]{1,2,0:T(8,128)(2,1)} async-done(((bf16[1,256,512]{1,2,0:T(8,128)(2,1)}), bf16[1,4096,512]{1,2,0:T(8,128)(2,1)}) %all-gather.10.cloned.1.call-update) | async-done | bytes 4194320 | tf_op jit(solution)/shard_map/all_gather | solution.py:36
  70.2 11.5 %fusion.57 = (f32[4,256]{1,0:T(4,128)S(1)}, f32[4,256,4096]{2,1,0:T(8,128)}) fusion(pred[256,4096]{1,0:T(8,128)(4,1)S(1)} %iota_compare_fusion, bf16[4096,4,128]{0,2,1:T(8,128)(2,1)} %bitcast.128, bf16[256,4,128]{2,1,0:T(4,128)(2,1)S(1)} %reshape.132), kind=kOutput, calls=%fused_computation.56 | convolution fusion | flops 1090523136 | bytes 22286336 | tf_op jit(solution)/shard_map/sub | solution.py:50
  81.7 6.9 %divide_convert_fusion = bf16[4,256,4096]{2,1,0:T(8,128)(2,1)S(1)} fusion(f32[4,256,4096]{2,1,0:T(8,128)} %get-tuple-element.22, f32[4,256]{1,0:T(4,128)S(1)} %get-tuple-element.21), kind=kLoop, calls=%fused_computation.1 | loop fusion | flops 8388608 | bytes 25169920 | tf_op jit(solution)/shard_map/convert_element_type | solution.py:51
  88.6 5.0 %fusion.62 = f32[4,4096,128]{1,2,0:T(8,128)} fusion(bf16[256,4,128]{0,2,1:T(8,128)(2,1)S(1)} %bitcast.127, bf16[4,256,4096]{2,1,0:T(8,128)(2,1)S(1)} %divide_convert_fusion), kind=kOutput, calls=%fused_computation.58 | convolution fusion | flops 1073741824 | bytes 17039360 | tf_op jit(solution)/shard_map/bhqk,bqhd->kbhd/dot_general | solution.py:55
  93.5 0.9 copy-done
  94.5 0.7 all-gather.8.cloned.1.call-update
  95.2 84.1 %reduce-scatter.3.cloned.1.call-done = f32[256,1,512]{0,2,1:T(8,128)} async-done(((f32[4096,1,512]{0,2,1:T(8,128)}), f32[256,1,512]{0,2,1:T(8,128)}) %reduce-scatter.3.cloned.1.call-update) | async-done | bytes 524304 | tf_op jit(solution)/shard_map/reduce_scatter | solution.py:56
  179.3 1.8 convert_element_type.51
  181.2 70.3 %all-gather.8.cloned.1.call-done = bf16[2,4096,512]{2,1,0:T(8,128)(2,1)} async-done(((bf16[2,256,512]{2,1,0:T(8,128)(2,1)}), bf16[2,4096,512]{2,1,0:T(8,128)(2,1)}) %all-gather.8.cloned.1.call-update) | async-done | bytes 8388624 | tf_op jit(solution)/shard_map/all_gather | solution.py:32
  251.5 3.6 fusion.7
  255.1 1.1 copy-done.4
  256.2 1.9 fusion.33
  258.1 7.4 %copy.67 = bf16[1,256,4096]{1,0,2:T(2,128)(2,1)} copy(bf16[1,256,4096]{2,1,0:T(8,128)(2,1)S(1)} %copy-done.1) | data formatting | bytes 4194304 | tf_op args[0]
  265.5 0.6 broadcast.42
  266.1 21.6 %reduce.7 = bf16[4096,256]{1,0:T(8,128)(2,1)S(1)} reduce(bf16[4096,1,256]{2,1,0:T(2,128)(2,1)} %bitcast.117, bf16[]{:T(256)} %broadcast.42), dimensions={1}, to_apply=%bitcast.100.reduce_sub_computation | reduce | bytes 4194306
  287.7 2.1 reshape.159
  289.8 5.7 %all-to-all-start.1 = ((bf16[16,2,32768]{2,1,0:T(2,128)(2,1)}), bf16[16,2,32768]{2,1,0:T(2,128)(2,1)S(1)}, u32[]{:S(2)}, u32[]{:S(2)}) async-start(bf16[16,2,32768]{2,1,0:T(2,128)(2,1)} %reshape.159), calls=%async_computation.3 | async-start | bytes 4194304 | tf_op jit(solution)/shard_map/all_to_all | solution.py:29
  295.6 0.6 dynamic-slice
  296.9 0.1 bitcast_dynamic-update-slice_fusion
  297.0 43.7 %all-reduce = s32[32]{0:T(128)S(1)} all-reduce(s32[32]{0:T(128)S(1)} %bitcast_dynamic-update-slice_fusion), channel_id=3, replica_groups=mesh['dp'=2,'sect'=16,'head'=4] {'sect'}, use_global_device_ids=true, to_apply=%add | all-reduce | flops 32 | bytes 256
  340.7 3.7 fusion.14
  344.4 1.9 fusion.6
  346.3 25.0 %copy.91 = bf16[1,4096,256]{2,0,1:T(2,128)(2,1)} copy(bf16[1,4096,256]{2,1,0:T(8,128)(2,1)S(1)} %fusion.6) | data formatting | bytes 4194304 | tf_op jit(solution)/shard_map/convert_element_type | solution.py:81
  371.4 22.9 %reduce.6 = bf16[4096,256]{1,0:T(8,128)(2,1)} reduce(bf16[4096,1,256]{2,1,0:T(2,128)(2,1)} %bitcast.118, bf16[]{:T(256)} %broadcast.42), dimensions={1}, to_apply=%bitcast.113.reduce_sub_computation | reduce | bytes 4194306
  394.3 4.0 reshape.161
  398.3 6.9 %all-to-all-start = ((bf16[16,2,32768]{2,1,0:T(2,128)(2,1)}), bf16[16,2,32768]{2,1,0:T(2,128)(2,1)}, u32[]{:S(2)}, u32[]{:S(2)}) async-start(bf16[16,2,32768]{2,1,0:T(2,128)(2,1)} %reshape.161), calls=%async_computation.1 | async-start | bytes 4194304 | tf_op jit(solution)/shard_map/all_to_all | solution.py:80
  405.2 6.8 %reshape.160 = bf16[4096,1,256]{2,1,0:T(2,128)(2,1)} reshape(bf16[16,2,32768]{2,1,0:T(2,128)(2,1)S(1)} %all-to-all-done.1) | data formatting | bytes 4194304
  411.9 2.5 copy.76
  414.5 2.4 copy.68
  416.9 4.2 fusion.36
  421.2 0.4 copy-done.6
  421.6 1.2 fusion.39
  422.8 0.8 pad_maximum_fusion
  423.7 0.3 reduce-scatter.5.cloned.1.call-start
  424.0 6.1 %all-to-all-done = bf16[16,2,32768]{2,1,0:T(2,128)(2,1)} async-done(((bf16[16,2,32768]{2,1,0:T(2,128)(2,1)}), bf16[16,2,32768]{2,1,0:T(2,128)(2,1)}, u32[]{:S(2)}, u32[]{:S(2)}) %all-to-all-start) | async-done | bytes 2097184 | tf_op jit(solution)/shard_map/all_to_all | solution.py:80
  430.1 10.5 %reshape.162 = bf16[4096,1,256]{2,1,0:T(2,128)(2,1)} reshape(bf16[16,2,32768]{2,1,0:T(2,128)(2,1)} %all-to-all-done) | data formatting | bytes 4194304
  440.6 2.5 copy.75
  443.1 2.4 copy.66
  445.5 6.5 %copy.73 = bf16[4096,512]{0,1:T(8,128)(2,1)} copy(bf16[4096,512]{1,0:T(8,128)(2,1)} %all-gather.12.cloned.1.call-done) | data formatting | bytes 8388608 | tf_op jit(solution)/shard_map/reshape.18
  452.0 7.6 %convolution_convert_fusion = bf16[4,128,256]{2,1,0:T(8,128)(2,1)S(1)} fusion(bf16[4096,4,128]{0,2,1:T(8,128)(2,1)} %bitcast.116, bf16[4,256,4096]{2,1,0:T(8,128)(2,1)} %copy-done), kind=kOutput, calls=%fused_computation.34 | convolution fusion | flops 1073872896 | bytes 12845056 | tf_op jit(solution)/shard_map/bhqk,bkhd->bqhd/dot_general | solution.py:52
  459.6 0.8 copy.69
  460.4 2.2 copy.71
  462.7 20.5 %reduce-scatter.5.cloned.1.call-done = bf16[1,256,1024]{1,2,0:T(8,128)(2,1)} async-done(((bf16[1,256,4096]{1,2,0:T(8,128)(2,1)}), bf16[1,256,1024]{1,2,0:T(8,128)(2,1)}) %reduce-scatter.5.cloned.1.call-update) | async-done | bytes 524304 | tf_op jit(solution)/shard_map/reduce_scatter | solution.py:83
  483.2 2.0 copy.70
  (37 shorter events, 0.6 us)
Async XLA Ops:
  7.2 63.0 %all-gather.10.cloned.1.call-start = ((), (), s32[]{:S(2)}) async-start(), calls=%async_computation.5 | async-start | bytes 4456448 | tf_op jit(solution)/shard_map/all_gather | solution.py:36
  9.0 170.3 %reduce-scatter.3.cloned.1.call-start = ((), (), s32[]{:S(2)}) async-start(), calls=%async_computation.6 | async-start | bytes 8912896 | tf_op jit(solution)/shard_map/reduce_scatter | solution.py:56
  88.6 5.9 %copy-start = (bf16[4,256,4096]{2,1,0:T(8,128)(2,1)}, bf16[4,256,4096]{2,1,0:T(8,128)(2,1)S(1)}, u32[]{:S(2)}) copy-start(bf16[4,256,4096]{2,1,0:T(8,128)(2,1)S(1)} %divide_convert_fusion) | copy-start | bytes 25165828
  94.4 86.8 %copy-start.7 = (s32[1,256]{1,0:T(1,128)S(1)}, s32[1,256]{1,0:T(1,128)}, u32[]{:S(2)}) copy-start(s32[1,256]{1,0:T(1,128)} %param.7) | copy-start | bytes 3076
  94.4 157.1 %copy-start.1 = (bf16[1,256,4096]{2,1,0:T(8,128)(2,1)S(1)}, bf16[1,256,4096]{2,1,0:T(8,128)(2,1)}, u32[]{:S(2)}) copy-start(bf16[1,256,4096]{2,1,0:T(8,128)(2,1)} %param.6) | copy-start | bytes 6291460
  94.5 157.1 %all-gather.8.cloned.1.call-start = ((), (), s32[]{:S(2)}) async-start(), calls=%async_computation.4 | async-start | bytes 8912896 | tf_op jit(solution)/shard_map/all_gather | solution.py:32
  95.2 245.5 %all-gather.14.cloned.1.call-start = ((), (), s32[]{:S(2)}) async-start(), calls=%async_computation.10 | async-start | bytes 4456448 | tf_op jit(solution)/shard_map/all_gather | solution.py:64
  181.1 264.4 %all-gather.12.cloned.1.call-start = ((), (), s32[]{:S(2)}) async-start(), calls=%async_computation.9 | async-start | bytes 4456448 | tf_op jit(solution)/shard_map/all_gather | solution.py:37
  251.5 4.6 copy-start.4
  287.7 7.9 %copy-start.8 = (u32[128]{0:T(128)S(1)}, u32[128]{0:T(128)}, u32[]{:S(2)}) copy-start(u32[128]{0:T(128)} %constant.29) | copy-start | bytes 1540
  287.7 53.0 %copy-start.3 = (bf16[2,256,512]{2,1,0:T(8,128)(2,1)S(1)}, bf16[2,256,512]{2,1,0:T(8,128)(2,1)}, u32[]{:S(2)}) copy-start(bf16[2,256,512]{2,1,0:T(8,128)(2,1)} %param.10) | copy-start | bytes 1572868
  289.8 108.5 %all-to-all-start.1 = ((bf16[16,2,32768]{2,1,0:T(2,128)(2,1)}), bf16[16,2,32768]{2,1,0:T(2,128)(2,1)S(1)}, u32[]{:S(2)}, u32[]{:S(2)}) async-start(bf16[16,2,32768]{2,1,0:T(2,128)(2,1)} %reshape.159), calls=%async_computation.3 | async-start | bytes 4194304 | tf_op jit(solution)/shard_map/all_to_all | solution.py:29
  340.7 3.7 copy-start.5
  398.3 31.8 %all-to-all-start = ((bf16[16,2,32768]{2,1,0:T(2,128)(2,1)}), bf16[16,2,32768]{2,1,0:T(2,128)(2,1)}, u32[]{:S(2)}, u32[]{:S(2)}) async-start(bf16[16,2,32768]{2,1,0:T(2,128)(2,1)} %reshape.161), calls=%async_computation.1 | async-start | bytes 4194304 | tf_op jit(solution)/shard_map/all_to_all | solution.py:80
  405.1 55.3 %all-reduce.3.cloned.1.call-start = ((), (), s32[]{:S(2)}) async-start(), calls=%async_computation.8 | async-start | bytes 1048576 | tf_op jit(solution)/shard_map/psum | solution.py:79
  416.9 4.3 copy-start.2
  416.9 4.7 copy-start.6
  423.7 59.5 %reduce-scatter.5.cloned.1.call-start = ((), (), s32[]{:S(2)}) async-start(), calls=%async_computation.7 | async-start | bytes 2621440 | tf_op jit(solution)/shard_map/reduce_scatter | solution.py:83
Sparse Core Ops, SparseCore 0:
  10.7 59.4 all-gather.9
  94.6 84.7 reduce-scatter.2
  181.5 69.9 all-gather.7
  254.1 77.2 all-gather.13
  334.0 54.4 all-gather.11
  423.8 25.5 all-reduce.2
  452.0 31.1 reduce-scatter.4
where the time goes:
time: 494 us; the launch traced here: 492 us
  waiting for transfers between devices  240 us (49%)
  local copies, waits for them, and re-layouts  84.9 us (17%)
  other arithmetic  54.7 us (11%)
  blocking collectives  43.7 us (9%)
  matrix products  40.7 us (8%)
  between operations  15 us (3%)
  starting transfers between devices  13.1 us (3%)
    reduce_scatter x1, waiting for transfers between devices, shards(): lax.psum_scatter(term.reshape(row_count * lax.axis_size('sect'), seq_coun...  84.1 us
    all_gather x1, waiting for transfers between devices, shards(): lax.all_gather(value_weight, 'sect', axis=1, tiled=True)  70.3 us
    all_gather x1, waiting for transfers between devices, shards(): lax.all_gather(key_rows, 'sect', axis=1, tiled=True)  58.3 us
    unnamed x34, local copies, waits for them, and re-layouts  46.4 us
    unnamed x2, other arithmetic  44.5 us
    unnamed x1, blocking collectives  43.7 us
    convert_element_type x1, local copies, waits for them, and re-layouts, shards(): input_part.astype(jnp.bfloat16)  25 us
    reduce_scatter x1, waiting for transfers between devices, shards(): lax.psum_scatter(regrouped.astype(jnp.bfloat16), 'head', scatter_dimensio...  20.5 us
  transfers between devices with their start and end apart: 9, of which 5 were waited for; matrix products, arithmetic and copies ran while one was open for 31% of the time, Pallas kernels for 0%

commit v1 on v0

v1 whole, which is shorter than its diff:
```python
import functools

import jax
import jax.numpy as jnp
from jax import lax
from jax.experimental import pallas as pl
from jax.experimental.pallas import tpu as pltpu
from jax.sharding import PartitionSpec as P

HD = 128
BLOCK = 128
SCALE = HD ** (-0.5)
EXP2_SCALE = SCALE * 1.4426950408889634
NEG = -1e30
MESH = pl.DeviceIdType.MESH
F32 = jnp.float32
BF16 = jnp.bfloat16

T = 256
C = 512
F = 1024
NH = C // HD


def dot(a, b, ca, cb):
    return lax.dot_general(a, b, (((ca,), (cb,)), ((), ())), preferred_element_type=F32)


def kernel(
    act, mod, qin, kin, win, gin,
    ctx_out, ig_out, wg_out,
    mod_v, mg, ag, wg, qg, gg, kg, vg,
    pt, st, gs,
    dvp, dvf, dvr, dv,
    vp, vf, vr,
    cp, cf, cr, co,
    ip, if_, ir, igs, igo,
    wother, wrecv, wown, wsend, wr, wo,
    loc_sem,
    s_mod, r_mod, s_act, r_act, s_actz, r_actz, s_k, r_k, s_q, r_q, s_g, r_g, s_w, r_w, s_wc, r_wc,
    s_st, r_st, s_dv, r_dv, s_dvg, r_dvg, s_v, r_v, s_vg, r_vg, s_c, r_c, s_i, r_i, s_t, r_t,
    s_wx, r_wx, s_wr, r_wr, s_wo, r_wo,
):
    c = lax.axis_index("dp")
    s = lax.axis_index("sect")
    z = lax.axis_index("head")
    y = s // 4
    x = lax.rem(s, 4)

    def wrap(v):
        return lax.rem(v + 4, 4)

    def on_x(d):
        return (c, y * 4 + wrap(x + d), z)

    def on_y(d):
        return (c, wrap(y + d) * 4 + x, z)

    def on_z(d):
        return (c, s, wrap(z + d))

    partner = (1 - c, s, z)
    across = (c, z * 4 + x, y)

    sends = []

    def remote(src, dst, ssem, rsem, dev):
        copy = pltpu.make_async_remote_copy(
            src_ref=src, dst_ref=dst, send_sem=ssem, recv_sem=rsem, device_id=dev, device_id_type=MESH
        )
        copy.start()
        sends.append(copy)
        return copy

    local = [
        pltpu.make_async_copy(mod, mod_v, loc_sem.at[0]),
        pltpu.make_async_copy(act.at[0, :, pl.ds(pl.multiple_of(y * F, F), F)], ag.at[y], loc_sem.at[1]),
        pltpu.make_async_copy(qin.at[0], qg.at[x], loc_sem.at[2]),
        pltpu.make_async_copy(kin.at[0], kg.at[y], loc_sem.at[3]),
        pltpu.make_async_copy(gin.at[0], gg.at[x], loc_sem.at[4]),
        pltpu.make_async_copy(win.at[0], wg.at[0, x], loc_sem.at[5]),
        pltpu.make_async_copy(win.at[1], wg.at[1, x], loc_sem.at[6]),
    ]
    for copy in local:
        copy.start()

    barrier = pltpu.get_barrier_semaphore()
    for d in (1, 2, 3):
        for dev in (on_x(d), on_y(d), on_z(d)):
            pl.semaphore_signal(barrier, inc=1, device_id=dev, device_id_type=MESH)
    pl.semaphore_signal(barrier, inc=1, device_id=partner, device_id_type=MESH)

    @pl.when(y != z)
    def _():
        pl.semaphore_signal(barrier, inc=1, device_id=across, device_id_type=MESH)

    pl.semaphore_wait(barrier, jnp.where(y != z, 11, 10))

    a_y, q_x, k_y, g_x, w_x = [], [], [], [], []
    quarter = pl.ds(pl.multiple_of(z * (T // 4), T // 4), T // 4)
    for d in (1, 3, 2):
        group = pl.ds(pl.multiple_of(wrap(y + d) * F, F), F)
        a_y.append(
            remote(act.at[0, quarter, group], ag.at[y, quarter], s_act.at[d - 1], r_act.at[d - 1], on_y(d))
        )
    for d in (1, 3, 2):
        q_x.append(remote(qin.at[0], qg.at[x], s_q.at[d - 1], r_q.at[d - 1], on_x(d)))
    for d in (1, 3, 2):
        k_y.append(remote(kin.at[0], kg.at[y], s_k.at[d - 1], r_k.at[d - 1], on_y(d)))

    local[0].wait()
    mg[y] = jnp.broadcast_to(mod_v[...], (8, T))
    m_y = [remote(mg.at[y], mg.at[y], s_mod.at[d - 1], r_mod.at[d - 1], on_y(d)) for d in (1, 2, 3)]

    a_z = []
    for n, d in enumerate((1, 3, 2)):
        a_y[n].wait_recv()
        piece = ag.at[wrap(y - d), quarter]
        for e in (1, 3, 2):
            a_z.append(remote(piece, piece, s_actz.at[d - 1, e - 1], r_actz.at[d - 1, e - 1], on_z(e)))

    for d in (1, 3, 2):
        g_x.append(remote(gin.at[0], gg.at[x], s_g.at[d - 1], r_g.at[d - 1], on_x(d)))
    for d in (1, 3, 2):
        w_x.append(remote(win.at[c], wg.at[c, x], s_w.at[d - 1], r_w.at[d - 1], on_x(d)))

    for copy in local[1:]:
        copy.wait()
    for copy in q_x + k_y:
        copy.wait_recv()

    key_pos = lax.broadcasted_iota(jnp.int32, (T, T), 0)
    query_pos = lax.broadcasted_iota(jnp.int32, (T, T), 1)
    ahead = query_pos - key_pos

    def score_block(p, _):
        cols = pl.ds(pl.multiple_of(p * T, T), T)
        for h in range(NH):
            hs = slice(h * HD, (h + 1) * HD)
            parts = []
            for q in range(4):
                sc = dot(kg[q, :, hs], qg[p, :, hs], 1, 1)
                parts.append(jnp.where(ahead >= (4 * q + x - 4 * y - p) * T, sc, NEG))
            top = functools.reduce(jnp.maximum, [jnp.max(v, axis=0, keepdims=True) for v in parts])
            total = jnp.zeros((1, T), F32)
            for q in range(4):
                pw = jnp.exp2((parts[q] - top) * EXP2_SCALE)
                total = total + jnp.sum(pw, axis=0, keepdims=True)
                pt[h, q * T:(q + 1) * T, cols] = pw.astype(BF16)
            st[x, h:h + 1, cols] = top
            st[x, NH + h:NH + h + 1, cols] = total
        return 0

    lax.fori_loop(0, 4, score_block, 0)
    st_x = [remote(st.at[x], st.at[x], s_st.at[d - 1], r_st.at[d - 1], on_x(d)) for d in (1, 3, 2)]
    for copy in st_x:
        copy.wait_recv()
    tops = [st[n, 0:NH, :] for n in range(4)]
    top = functools.reduce(jnp.maximum, tops)
    total = jnp.zeros_like(top)
    for n in range(4):
        total = total + st[n, NH:2 * NH, :] * jnp.exp2((tops[n] - top) * EXP2_SCALE)
    factor = jnp.exp2((st[x, 0:NH, :] - top) * EXP2_SCALE) / total

    for copy in g_x:
        copy.wait_recv()
    for h in range(NH):
        hs = slice(h * HD, (h + 1) * HD)
        for p in range(4):
            wide = jnp.broadcast_to(factor[h:h + 1, p * T:(p + 1) * T], (HD, T)).T
            gs[p * T:(p + 1) * T, hs] = (gg[p, :, hs].astype(F32) * wide).astype(BF16)

    dv_y = []
    for e in (1, 3, 2, 0):
        q = wrap(y + e)
        rows = pl.ds(pl.multiple_of(q * T, T), T)
        for h in range(NH):
            hs = slice(h * HD, (h + 1) * HD)
            part = dot(pt[h, rows, :], gs[:, hs], 1, 0)
            if e:
                dvp[e - 1, :, hs] = part.astype(BF16)
            else:
                dvf[:, hs] = part
        if e:
            dv_y.append(remote(dvp.at[e - 1], dvr.at[e - 1], s_dv.at[e - 1], r_dv.at[e - 1], on_y(e)))

    w_c = []
    for n, d in enumerate((1, 3, 2)):
        w_x[n].wait_recv()
        block = wg.at[c, wrap(x - d)]
        w_c.append(remote(block, block, s_wc.at[d - 1], r_wc.at[d - 1], partner))
    for copy in m_y + a_z:
        copy.wait_recv()
    for copy in w_c:
        copy.wait_recv()

    def image_rows(q, width):
        parts = []
        for b in range(T // BLOCK):
            row = mg[q, 0:1, b * BLOCK:(b + 1) * BLOCK]
            row = jnp.concatenate([row] * (width // BLOCK), axis=1)
            parts.append(jnp.broadcast_to(row, (BLOCK, width)))
        return jnp.concatenate(parts, axis=0) == 1

    def value_part(q):
        rows = ag[q]
        text = dot(rows, wg[0].reshape(F, C), 1, 0)
        image = dot(rows, wg[1].reshape(F, C), 1, 0)
        return jnp.where(image_rows(q, C), image, text)

    v_y = []
    for e in (1, 3, 2, 0):
        part = value_part(wrap(y + e))
        if e:
            vp[e - 1] = part.astype(BF16)
            v_y.append(remote(vp.at[e - 1], vr.at[e - 1], s_v.at[e - 1], r_v.at[e - 1], on_y(e)))
        else:
            vf[...] = part

    for copy in dv_y:
        copy.wait_recv()
    dv[y] = (dvf[...] + dvr[0].astype(F32) + dvr[1].astype(F32) + dvr[2].astype(F32)).astype(BF16)
    dvg_y = [remote(dv.at[y], dv.at[y], s_dvg.at[d - 1], r_dvg.at[d - 1], on_y(d)) for d in (1, 3, 2)]
    for copy in v_y:
        copy.wait_recv()
    vg[y] = (vf[...] + vr[0].astype(F32) + vr[1].astype(F32) + vr[2].astype(F32)).astype(BF16)
    vg_y = [remote(vg.at[y], vg.at[y], s_vg.at[d - 1], r_vg.at[d - 1], on_y(d)) for d in (1, 3, 2)]

    for copy in dvg_y:
        copy.wait_recv()

    def back_part(q):
        rows = dv[q]
        text = dot(rows, wg[0].reshape(F, C), 1, 1)
        image = dot(rows, wg[1].reshape(F, C), 1, 1)
        return jnp.where(image_rows(q, F), image, text)

    i_z = []
    for e in (1, 3, 2, 0):
        part = back_part(wrap(z + e))
        if e:
            ip[e - 1] = part.astype(BF16)
            i_z.append(remote(ip.at[e - 1], ir.at[e - 1], s_i.at[e - 1], r_i.at[e - 1], on_z(e)))
        else:
            if_[...] = part

    feats = ag[...].reshape(4 * T, F)

    def update(kind):
        masked = [
            jnp.where(image_rows(q, C) == (kind == 1), dv[q].astype(F32), 0.0).astype(BF16) for q in range(4)
        ]
        return dot(feats, jnp.concatenate(masked, axis=0), 0, 0)

    wother[...] = update(1 - c).astype(BF16)
    wx = remote(wother, wrecv, s_wx.at[0], r_wx.at[0], partner)
    wown[...] = update(c)
    wx.wait_recv()
    wr_x = []
    for e in (1, 3, 2, 0):
        rows = pl.ds(pl.multiple_of(wrap(x + e) * T, T), T)
        summed = wown[rows, :] + wrecv[rows, :].astype(F32)
        if e:
            wsend[e - 1] = summed.astype(BF16)
            wr_x.append(remote(wsend.at[e - 1], wr.at[e - 1], s_wr.at[e - 1], r_wr.at[e - 1], on_x(e)))
        else:
            own_update = summed
            wo[c] = own_update

    for copy in vg_y:
        copy.wait_recv()
    values = vg[...].reshape(4 * T, C)
    c_x = []
    for e in (1, 3, 2, 0):
        p = wrap(x + e)
        cols = pl.ds(pl.multiple_of(p * T, T), T)
        for h in range(NH):
            hs = slice(h * HD, (h + 1) * HD)
            part = dot(values[:, hs], pt[h, :, cols], 0, 0)
            top_p = functools.reduce(jnp.maximum, [st[n, h:h + 1, cols] for n in range(4)])
            total_p = jnp.zeros_like(top_p)
            for n in range(4):
                total_p = total_p + st[n, NH + h:NH + h + 1, cols] * jnp.exp2(
                    (st[n, h:h + 1, cols] - top_p) * EXP2_SCALE
                )
            factor_p = jnp.exp2((st[x, h:h + 1, cols] - top_p) * EXP2_SCALE) / total_p
            part = (part * factor_p).T
            if e:
                cp[e - 1, :, hs] = part.astype(BF16)
            else:
                cf[:, hs] = part
        if e:
            c_x.append(remote(cp.at[e - 1], cr.at[e - 1], s_c.at[e - 1], r_c.at[e - 1], on_x(e)))

    for copy in i_z:
        copy.wait_recv()
    summed = (if_[...] + ir[0].astype(F32) + ir[1].astype(F32) + ir[2].astype(F32)).astype(BF16)

    @pl.when(y == z)
    def _():
        igo[...] = summed

    @pl.when(y != z)
    def _():
        igs[...] = summed
        pltpu.make_async_remote_copy(
            src_ref=igs, dst_ref=igo, send_sem=s_t.at[0], recv_sem=r_t.at[0], device_id=across, device_id_type=MESH
        ).start()

    for copy in wr_x:
        copy.wait_recv()
    wo[c] = wo[c] + wr[0].astype(F32) + wr[1].astype(F32) + wr[2].astype(F32)
    w_out = remote(wo.at[c], wo.at[c], s_wo.at[0], r_wo.at[0], partner)

    for copy in c_x:
        copy.wait_recv()
    co[...] = (cf[...] + cr[0].astype(F32) + cr[1].astype(F32) + cr[2].astype(F32)).astype(BF16)
    out_c = pltpu.make_async_copy(co, ctx_out, loc_sem.at[0])
    out_c.start()

    @pl.when(y != z)
    def _():
        copy = pltpu.make_async_remote_copy(
            src_ref=igs, dst_ref=igo, send_sem=s_t.at[0], recv_sem=r_t.at[0], device_id=across, device_id_type=MESH
        )
        copy.wait()

    out_i = pltpu.make_async_copy(igo, ig_out, loc_sem.at[1])
    out_i.start()
    w_out.wait_recv()
    out_w = pltpu.make_async_copy(wo, wg_out, loc_sem.at[2])
    out_w.start()
    for copy in sends:
        copy.wait_send()
    out_c.wait()
    out_i.wait()
    out_w.wait()


def shards(activations, modality, query_rows, key_rows, value_weight, context_grad):
    vm = lambda shape, dtype=BF16: pltpu.VMEM(shape, dtype)
    dma = lambda *shape: pltpu.SemaphoreType.DMA(shape)
    any_spec = pl.BlockSpec(memory_space=pl.ANY)
    three = [dma(3), dma(3)]
    ctx, ig, wgrad = pl.pallas_call(
        kernel,
        out_shape=(
            jax.ShapeDtypeStruct((T, C), BF16),
            jax.ShapeDtypeStruct((T, F), BF16),
            jax.ShapeDtypeStruct((2, T, C), F32),
        ),
        in_specs=[any_spec] * 6,
        out_specs=(any_spec,) * 3,
        scratch_shapes=[
            vm((1, T), jnp.int32), vm((4, 8, T), jnp.int32), vm((4, T, F)), vm((2, 4, T, C)),
            vm((4, T, C)), vm((4, T, C)), vm((4, T, C)), vm((4, T, C)),
            vm((NH, 4 * T, 4 * T)), vm((4, 8, 4 * T), F32), vm((4 * T, C)),
            vm((3, T, C)), vm((T, C), F32), vm((3, T, C)), vm((4, T, C)),
            vm((3, T, C)), vm((T, C), F32), vm((3, T, C)),
            vm((3, T, C)), vm((T, C), F32), vm((3, T, C)), vm((T, C)),
            vm((3, T, F)), vm((T, F), F32), vm((3, T, F)), vm((T, F)), vm((T, F)),
            vm((F, C)), vm((F, C)), vm((F, C), F32), vm((3, T, C)), vm((3, T, C)), vm((2, T, C), F32),
            dma(7),
            *three, *three, dma(3, 3), dma(3, 3), *three, *three, *three, *three, *three,
            *three, *three, *three, *three, *three, *three, *three, dma(1), dma(1),
            dma(1), dma(1), *three, dma(1), dma(1),
        ],
        compiler_params=pltpu.CompilerParams(
            collective_id=0, has_side_effects=True, vmem_limit_bytes=60 * 2**20
        ),
        name="routed_attention",
    )(activations, modality, query_rows, key_rows, value_weight, context_grad)
    return ctx[None], ig[None], wgrad


def solution(mesh):
    return jax.shard_map(
        shards,
        mesh=mesh,
        in_specs=(
            P("dp", "sect", None),
            P("dp", "sect"),
            P("dp", "sect", "head"),
            P("dp", "sect", "head"),
            P(None, "sect", "head"),
            P("dp", "sect", "head"),
        ),
        out_specs=(P("dp", "sect", "head"), P("dp", "sect", "head"), P(None, "sect", "head")),
        check_vma=False,
    )
```

time: 494 us -> 146 us (0.30)
  the two profiles are of different devices: /device:TPU:2 before, /device:TPU:108 now
where the time goes in v1:
time: 146 us; the launch traced here: 145 us
  Pallas kernels  140 us (96%)
  local copies, waits for them, and re-layouts  4.6 us (3%)
    pallas_call x1, Pallas kernels, shards(): pl.pallas_call(kernel, out_shape=(jax.ShapeDtypeStruct((T, C), BF16), jax...  140 us
    unnamed x5, local copies, waits for them, and re-layouts  4.6 us

profile of v1, /device:TPU:108, one launch (start us, length us, event | category | flops | bytes accessed | tf_op | source)
XLA Modules:
  0.0 145.4 jit_solution(9041501802586446053)
XLA Ops:
  0.6 140.2 %routed_attention.1 = (bf16[256,512]{1,0:T(8,128)(2,1)}, bf16[256,1024]{1,0:T(8,128)(2,1)}, f32[2,256,512]{2,1,0:T(8,128)}) custom-call(bf16[1,256,4096]{2,1,0:T(8,128)(2,1)} %act.1, s32[1,256]{1,0:T(1,128)} %mod.1, bf16[1,256,512]{2,1,0:T(8,128)(2,1)} %qin.1, bf16[1,256,512]{2,1,0:T(8,128)(2,1)} %kin.1, bf16[2,256,512]{2,1,0:T(8,128)(2,1)} %win.1, ...), custom_call_target="tpu_custom_call" | custom-call | tf_op jit(solution)/shard_map/routed_attention/pallas_call | solution.py:345
  140.8 0.0 copy-start
  140.8 1.8 %copy.12 = bf16[1,256,512]{2,1,0:T(8,128)(2,1)} copy(bf16[1,256,512]{2,1,0:T(8,128)(2,1)} %bitcast.3) | data formatting | bytes 524288
  142.6 1.9 %copy.13 = bf16[1,256,1024]{2,1,0:T(8,128)(2,1)} copy(bf16[1,256,1024]{2,1,0:T(8,128)(2,1)} %bitcast.2) | data formatting | bytes 1048576
  144.4 0.0 copy-done
  144.5 1.0 copy.14
Async XLA Ops:
  140.8 3.6 %copy-start = (f32[2,256,512]{2,1,0:T(8,128)S(1)}, f32[2,256,512]{2,1,0:T(8,128)}, u32[]{:S(2)}) copy-start(f32[2,256,512]{2,1,0:T(8,128)} %get-tuple-element.14) | copy-start | bytes 3145732

commit v2 on v0

v2 whole, which is shorter than its diff:
```python
import functools

import jax
import jax.numpy as jnp
from jax import lax
from jax.experimental import pallas as pl
from jax.experimental.pallas import tpu as pltpu
from jax.sharding import PartitionSpec as P

HD = 128
BLOCK = 128
EXP2_SCALE = HD ** (-0.5) * 1.4426950408889634
NEG = -1e30
MESH = pl.DeviceIdType.MESH
F32 = jnp.float32
BF16 = jnp.bfloat16

T = 256
C = 512
F = 1024
FB = 256
NH = C // HD


def dot(a, b, ca, cb):
    return lax.dot_general(a, b, (((ca,), (cb,)), ((), ())), preferred_element_type=F32)


def wrap(v):
    return lax.rem(v + 4, 4)


def kernel(
    act, mod, qin, kin, win, gin,
    ctx_out, ig_out, wg_out,
    mod_v, mg, ag, wg, qg, gg, kg, vg, dv,
    pt, st, fa, gs,
    d_part, d_in, d_own,
    v_part, v_in, v_own,
    c_part, c_in, c_own, co,
    i_part, i_in, i_own, igs, igo,
    w_other, w_recv, w_own, w_mine, w_part, w_in, wo,
    loc_sem, sems, ssem_t, rsem_t,
):
    c = lax.axis_index("dp")
    s = lax.axis_index("sect")
    z = lax.axis_index("head")
    y = s // 4
    x = lax.rem(s, 4)

    def on_x(d):
        return (c, y * 4 + wrap(x + d), z)

    def on_y(d):
        return (c, wrap(y + d) * 4 + x, z)

    def on_z(d):
        return (c, s, wrap(z + d))

    partner = (1 - c, s, z)
    sends = []
    used = [0]

    def remote(src, dst, dev):
        n = used[0]
        used[0] += 1
        copy = pltpu.make_async_remote_copy(
            src_ref=src, dst_ref=dst, send_sem=sems.at[0, n], recv_sem=sems.at[1, n],
            device_id=dev, device_id_type=MESH,
        )
        copy.start()
        sends.append(copy)
        return copy

    class Gather:
        def __init__(self, on, slot, fixed=False):
            self.on, self.slot, self.fixed = on, slot, fixed

        def there(self, d, part, step):
            return self.slot(d, part) if self.fixed else self.slot((d + step) % 4, part)

        def start(self, own=None):
            on, there = self.on, self.there
            own = own or (lambda part: self.slot(0, part))
            self.a_up = remote(own(0), there(0, 0, 1), on(1))
            self.b_dn = remote(own(1), there(0, 1, -1), on(-1))
            self.b_up = remote(own(1), there(0, 1, 1), on(1))
            self.a_dn = remote(own(0), there(0, 0, -1), on(-1))

        def relay(self):
            on, there = self.on, self.there
            self.a_up.wait_recv()
            self.a_far = remote(self.slot(1, 0), there(1, 0, 1), on(1))
            self.b_dn.wait_recv()
            self.b_far = remote(self.slot(3, 1), there(3, 1, -1), on(-1))

        def finish(self):
            for copy in (self.b_up, self.a_dn, self.a_far, self.b_far):
                copy.wait_recv()

    def gather(on, buf, rows):
        half = rows // 2
        return Gather(on, lambda d, part: buf.at[d, pl.ds(part * half, half)])

    class Sum:
        def __init__(self, on, part, inbox, half):
            self.on, self.part, self.inbox, self.half = on, part, inbox, half
            self.a, self.b = pl.ds(0, half), pl.ds(half, half)

        def far(self):
            self.f_up = remote(self.part.at[1, self.a], self.inbox.at[0], self.on(1))
            self.f_dn = remote(self.part.at[1, self.b], self.inbox.at[1], self.on(-1))

        def near_up(self):
            self.n_up = remote(self.part.at[0, self.b], self.inbox.at[2], self.on(1))

        def near_dn(self):
            self.n_dn = remote(self.part.at[2, self.a], self.inbox.at[3], self.on(-1))

        def relay(self):
            self.f_up.wait_recv()
            self.part[0, self.a] = (self.part[0, self.a].astype(F32) + self.inbox[0].astype(F32)).astype(BF16)
            self.s_up = remote(self.part.at[0, self.a], self.inbox.at[4], self.on(1))
            self.f_dn.wait_recv()
            self.part[2, self.b] = (self.part[2, self.b].astype(F32) + self.inbox[1].astype(F32)).astype(BF16)
            self.s_dn = remote(self.part.at[2, self.b], self.inbox.at[5], self.on(-1))

        def finish(self, own):
            for copy in (self.n_up, self.n_dn, self.s_up, self.s_dn):
                copy.wait_recv()
            first = own[self.a] + self.inbox[4].astype(F32) + self.inbox[3].astype(F32)
            second = own[self.b] + self.inbox[2].astype(F32) + self.inbox[5].astype(F32)
            return first, second

    local = [
        pltpu.make_async_copy(mod, mod_v, loc_sem.at[0]),
        pltpu.make_async_copy(act.at[0, :, pl.ds(pl.multiple_of(y * F, F), F)], ag.at[0], loc_sem.at[1]),
        pltpu.make_async_copy(qin.at[0], qg.at[0], loc_sem.at[2]),
        pltpu.make_async_copy(kin.at[0], kg.at[0], loc_sem.at[3]),
        pltpu.make_async_copy(gin.at[0], gg.at[0], loc_sem.at[4]),
        pltpu.make_async_copy(win.at[0], wg.at[0, x], loc_sem.at[5]),
        pltpu.make_async_copy(win.at[1], wg.at[1, x], loc_sem.at[6]),
    ]
    for copy in local:
        copy.start()

    barrier = pltpu.get_barrier_semaphore()
    for d in (1, 2, 3):
        for dev in (on_x(d), on_y(d), on_z(d)):
            pl.semaphore_signal(barrier, inc=1, device_id=dev, device_id_type=MESH)
    pl.semaphore_signal(barrier, inc=1, device_id=partner, device_id_type=MESH)
    for n in range(4):

        @pl.when(jnp.logical_and(n != y, y != z))
        def _(n=n):
            pl.semaphore_signal(barrier, inc=1, device_id=(c, n * 4 + x, y), device_id_type=MESH)

        @pl.when(jnp.logical_and(n != z, y != z))
        def _(n=n):
            pl.semaphore_signal(barrier, inc=1, device_id=(c, z * 4 + x, n), device_id_type=MESH)

    pl.semaphore_wait(barrier, jnp.where(y != z, 16, 10))

    def hbm_half(ref):
        return lambda part: ref.at[0, pl.ds(part * (T // 2), T // 2)]

    q_all, k_all = gather(on_x, qg, T), gather(on_y, kg, T)
    g_all = gather(on_x, gg, T)
    k_all.start(hbm_half(kin))
    q_all.start(hbm_half(qin))

    local[0].wait()
    mg[0] = jnp.broadcast_to(mod_v[...], (8, T))
    m_y = [remote(mg.at[0], mg.at[d], on_y(d)) for d in (1, 2, 3)]
    k_all.relay()
    q_all.relay()
    for copy in local[1:]:
        copy.wait()
    k_all.finish()
    q_all.finish()

    g_all.start(hbm_half(gin))
    quarter = pl.ds(pl.multiple_of(z * (T // 4), T // 4), T // 4)
    a_y = []
    for d in (1, 3, 2):
        group = pl.ds(pl.multiple_of(wrap(y + d) * F, F), F)
        a_y.append(remote(act.at[0, quarter, group], ag.at[d, quarter], on_y(d)))

    key_pos = lax.broadcasted_iota(jnp.int32, (T, T), 0)
    query_pos = lax.broadcasted_iota(jnp.int32, (T, T), 1)
    ahead = query_pos - key_pos

    def score_block(a, _):
        p = wrap(x - a)
        cols = pl.ds(pl.multiple_of(a * T, T), T)
        for h in range(NH):
            hs = slice(h * HD, (h + 1) * HD)
            parts = []
            for b in range(4):
                sc = dot(kg[b, :, hs], qg[a, :, hs], 1, 1)
                parts.append(jnp.where(ahead >= (4 * wrap(y - b) + x - 4 * y - p) * T, sc, NEG))
            top = functools.reduce(jnp.maximum, [jnp.max(v, axis=0, keepdims=True) for v in parts])
            total = jnp.zeros((1, T), F32)
            for b in range(4):
                pw = jnp.exp2((parts[b] - top) * EXP2_SCALE)
                total = total + jnp.sum(pw, axis=0, keepdims=True)
                pt[h, b * T:(b + 1) * T, cols] = pw.astype(BF16)
            st[0, p, h:h + 1, :] = top
            st[0, p, NH + h:NH + h + 1, :] = total
        return 0

    lax.fori_loop(0, 2, score_block, 0)
    g_all.relay()
    lax.fori_loop(2, 4, score_block, 0)
    st_x = [remote(st.at[0], st.at[d], on_x(d)) for d in (1, 3, 2)]

    w_all = Gather(on_x, lambda d, part: wg.at[c, wrap(x - d), pl.ds(part * (FB // 2), FB // 2)], fixed=True)
    w_all.start(lambda part: win.at[c, pl.ds(part * (FB // 2), FB // 2)])
    for copy in a_y:
        copy.wait_recv()

    def z_slot(d, part):
        rows = pl.ds(pl.multiple_of(wrap(z - d) * (T // 4) + part * (T // 8), T // 8), T // 8)
        return ag.at[pl.ds(1, 3), rows]

    a_all = Gather(on_z, z_slot, fixed=True)
    a_all.start()

    for copy in st_x:
        copy.wait_recv()
    for a in range(4):
        p = wrap(x - a)
        tops = [st[d, p, 0:NH] for d in range(4)]
        top = functools.reduce(jnp.maximum, tops)
        total = jnp.zeros_like(top)
        for d in range(4):
            total = total + st[d, p, NH:2 * NH] * jnp.exp2((tops[d] - top) * EXP2_SCALE)
        each = jnp.exp2((tops[0] - top) * EXP2_SCALE) / total
        for h in range(NH):
            fa[a, h] = jnp.broadcast_to(each[h:h + 1], (8, T))

    def factor(a, h):
        return jnp.concatenate([fa[a, h]] * (HD // 8), axis=0)

    g_all.finish()
    for h in range(NH):
        hs = slice(h * HD, (h + 1) * HD)
        for a in range(4):
            wide = factor(a, h).T
            gs[a * T:(a + 1) * T, hs] = (gg[a, :, hs].astype(F32) * wide).astype(BF16)

    d_sum = Sum(on_y, d_part, d_in, T // 2)

    def d_block(e):
        b = (4 - e) % 4
        for h in range(NH):
            hs = slice(h * HD, (h + 1) * HD)
            part = dot(pt[h, b * T:(b + 1) * T, :], gs[:, hs], 1, 0)
            if e:
                d_part[e - 1, :, hs] = part.astype(BF16)
            else:
                d_own[:, hs] = part

    d_block(2)
    d_sum.far()
    d_block(1)
    d_sum.near_up()
    d_block(3)
    d_sum.near_dn()
    a_all.relay()
    d_block(0)
    w_all.relay()
    d_sum.relay()
    w_all.finish()
    w_c = [remote(wg.at[c, wrap(x - d)], wg.at[c, wrap(x - d)], partner) for d in (1, 2, 3)]
    first, second = d_sum.finish(d_own)
    dv[0, 0:T // 2] = first.astype(BF16)
    dv[0, T // 2:T] = second.astype(BF16)
    d_all = gather(on_y, dv, T)
    d_all.start()

    def image_rows(b, width):
        parts = []
        for n in range(T // BLOCK):
            tile = mg[b, :, n * BLOCK:(n + 1) * BLOCK]
            tile = jnp.concatenate([tile] * (width // BLOCK), axis=1)
            parts += [tile] * (BLOCK // 8)
        return jnp.concatenate(parts, axis=0) == 1

    a_all.finish()
    for copy in (*m_y, *w_c):
        copy.wait_recv()
    v_sum = Sum(on_y, v_part, v_in, T // 2)

    def v_block(e):
        b = (4 - e) % 4
        rows = ag[b]
        text = dot(rows, wg[0].reshape(F, C), 1, 0)
        image = dot(rows, wg[1].reshape(F, C), 1, 0)
        part = jnp.where(image_rows(b, C), image, text)
        if e:
            v_part[e - 1] = part.astype(BF16)
        else:
            v_own[...] = part

    v_block(2)
    v_block(1)
    d_all.relay()
    v_sum.far()
    v_sum.near_up()
    v_block(3)
    v_sum.near_dn()
    v_block(0)
    d_all.finish()

    i_sum = Sum(on_z, i_part, i_in, 2 * T)

    def i_block(e):
        n = wrap(z + e)
        for b in range(4):
            rows = dv[b]
            text = dot(rows, wg[0, n], 1, 1)
            image = dot(rows, wg[1, n], 1, 1)
            part = jnp.where(image_rows(b, FB), image, text)
            if e:
                i_part[e - 1, b * T:(b + 1) * T] = part.astype(BF16)
            else:
                i_own[b * T:(b + 1) * T] = part

    i_block(2)
    i_sum.far()
    i_block(1)
    i_sum.near_up()
    i_block(3)
    i_sum.near_dn()
    i_block(0)

    feats = ag[...].reshape(4 * T, F)

    def update(kind):
        masked = [
            jnp.where(image_rows(b, C) == (kind == 1), dv[b].astype(F32), 0.0).astype(BF16) for b in range(4)
        ]
        return dot(feats, jnp.concatenate(masked, axis=0), 0, 0)

    w_other[...] = update(1 - c).astype(BF16)
    w_x = remote(w_other, w_recv, partner)
    v_sum.relay()
    i_sum.relay()
    w_own[...] = update(c)
    first, second = v_sum.finish(v_own)
    vg[0, 0:T // 2] = first.astype(BF16)
    vg[0, T // 2:T] = second.astype(BF16)
    v_all = gather(on_y, vg, T)
    v_all.start()

    w_x.wait_recv()
    w_sum = Sum(on_x, w_part, w_in, FB // 2)
    for e in (2, 1, 3, 0):
        rows = pl.ds(pl.multiple_of(wrap(x + e) * FB, FB), FB)
        summed = w_own[rows, :] + w_recv[rows, :].astype(F32)
        if e:
            w_part[e - 1] = summed.astype(BF16)
            (w_sum.near_up, w_sum.far, w_sum.near_dn)[e - 1]()
        else:
            w_mine[...] = summed
    v_all.relay()
    w_sum.relay()

    first, second = i_sum.finish(i_own)
    for b, rows in ((0, first[0:T]), (1, first[T:2 * T]), (2, second[0:T]), (3, second[T:2 * T])):
        igs[b] = rows.astype(BF16)
    cols = pl.ds(pl.multiple_of(z * FB, FB), FB)

    def last_move(b, action):
        n = wrap(y - b)
        copy = pltpu.make_async_remote_copy(
            src_ref=igs.at[b], dst_ref=igo.at[:, cols], send_sem=ssem_t.at[b], recv_sem=rsem_t.at[z],
            device_id=(c, n * 4 + x, y), device_id_type=MESH,
        )
        action(copy)

    for b in (1, 2, 3):
        last_move(b, lambda copy: copy.start())

    @pl.when(y != z)
    def _():
        last_move(0, lambda copy: copy.start())

    @pl.when(y == z)
    def _():
        igo[:, cols] = igs[0]

    v_all.finish()
    values = vg[...].reshape(4 * T, C)
    c_sum = Sum(on_x, c_part, c_in, T // 2)

    def c_block(e):
        a = (4 - e) % 4
        for h in range(NH):
            hs = slice(h * HD, (h + 1) * HD)
            part = dot(values[:, hs], pt[h, :, a * T:(a + 1) * T], 0, 0)
            part = (part * factor(a, h)).T
            if e:
                c_part[e - 1, :, hs] = part.astype(BF16)
            else:
                c_own[:, hs] = part

    c_block(2)
    c_sum.far()
    c_block(1)
    c_sum.near_up()
    c_block(3)
    c_sum.near_dn()
    c_block(0)

    first, second = w_sum.finish(w_mine)
    wo[c, 0:FB // 2] = first
    wo[c, FB // 2:FB] = second
    w_out = remote(wo.at[c], wo.at[c], partner)
    c_sum.relay()
    w_out.wait_recv()
    out_w = pltpu.make_async_copy(wo, wg_out, loc_sem.at[2])
    out_w.start()

    for n in range(4):

        @pl.when(jnp.logical_or(y != z, n != z))
        def _(n=n):
            pltpu.make_async_remote_copy(
                src_ref=igs.at[0], dst_ref=igo.at[:, n * FB:(n + 1) * FB], send_sem=ssem_t.at[0], recv_sem=rsem_t.at[n],
                device_id=(c, s, wrap(z + 1)), device_id_type=MESH,
            ).wait_recv()

    out_i = pltpu.make_async_copy(igo, ig_out, loc_sem.at[1])
    out_i.start()
    first, second = c_sum.finish(c_own)
    co[0:T // 2] = first.astype(BF16)
    co[T // 2:T] = second.astype(BF16)
    out_c = pltpu.make_async_copy(co, ctx_out, loc_sem.at[0])
    out_c.start()
    for copy in sends:
        copy.wait_send()
    for b in (1, 2, 3):
        last_move(b, lambda copy: copy.wait_send())

    @pl.when(y != z)
    def _():
        last_move(0, lambda copy: copy.wait_send())

    out_c.wait()
    out_i.wait()
    out_w.wait()


def shards(activations, modality, query_rows, key_rows, value_weight, context_grad):
    vm = lambda shape, dtype=BF16: pltpu.VMEM(shape, dtype)
    dma = lambda *shape: pltpu.SemaphoreType.DMA(shape)
    any_spec = pl.BlockSpec(memory_space=pl.ANY)
    ring_sum = lambda rows, cols: [vm((3, rows, cols)), vm((6, rows // 2, cols)), vm((rows, cols), F32)]
    ctx, ig, wgrad = pl.pallas_call(
        kernel,
        out_shape=(
            jax.ShapeDtypeStruct((T, C), BF16),
            jax.ShapeDtypeStruct((T, F), BF16),
            jax.ShapeDtypeStruct((2, T, C), F32),
        ),
        in_specs=[any_spec] * 6,
        out_specs=(any_spec,) * 3,
        scratch_shapes=[
            vm((1, T), jnp.int32), vm((4, 8, T), jnp.int32), vm((4, T, F)), vm((2, 4, FB, C)),
            vm((4, T, C)), vm((4, T, C)), vm((4, T, C)), vm((4, T, C)), vm((4, T, C)),
            vm((NH, 4 * T, 4 * T)), vm((4, 4, 8, T), F32), vm((4, NH, 8, T), F32), vm((4 * T, C)),
            *ring_sum(T, C), *ring_sum(T, C), *ring_sum(T, C), vm((T, C)),
            *ring_sum(4 * T, FB), vm((4, T, FB)), vm((T, F)),
            vm((F, C)), vm((F, C)), vm((F, C), F32), vm((FB, C), F32), vm((3, FB, C)), vm((6, FB // 2, C)), vm((2, FB, C), F32),
            dma(7), dma(2, 96), dma(4), dma(4),
        ],
        compiler_params=pltpu.CompilerParams(
            collective_id=0, has_side_effects=True, vmem_limit_bytes=60 * 2**20
        ),
        name="routed_attention",
    )(activations, modality, query_rows, key_rows, value_weight, context_grad)
    return ctx[None], ig[None], wgrad


def solution(mesh):
    return jax.shard_map(
        shards,
        mesh=mesh,
        in_specs=(
            P("dp", "sect", None),
            P("dp", "sect"),
            P("dp", "sect", "head"),
            P("dp", "sect", "head"),
            P(None, "sect", "head"),
            P("dp", "sect", "head"),
        ),
        out_specs=(P("dp", "sect", "head"), P("dp", "sect", "head"), P(None, "sect", "head")),
        check_vma=False,
    )
```

time: 494 us -> 92.7 us (0.19)
  waiting for transfers between devices: 240 us -> 0 us
  Pallas kernels: 0 us -> 87.3 us
  local copies, waits for them, and re-layouts: 84.9 us -> 4.6 us
  other arithmetic: 54.7 us -> 0 us
  blocking collectives: 43.7 us -> 0 us
  matrix products: 40.7 us -> 0 us
  between operations: 15 us -> 0.65 us
  starting transfers between devices: 13.1 us -> 0 us
    all_gather x4 -> x0, waiting for transfers between devices: 129 us -> none  [the longest x1 70.3 us: shards(): lax.all_gather(value_weight, 'sect', axis=1, tiled=True)]
    reduce_scatter x2 -> x0, waiting for transfers between devices: 105 us -> none  [the longest x1 84.1 us: shards(): lax.psum_scatter(term.reshape(row_count * lax.axis_size('sect'), seq_coun...]
    pallas_call x0 -> x1, Pallas kernels: none -> 87.3 us  [shards(): pl.pallas_call(kernel, out_shape=(jax.ShapeDtypeStruct((T, C), BF16), jax...]
    unnamed x2 -> x0, other arithmetic: 44.5 us -> none
    unnamed x1 -> x0, blocking collectives: 43.7 us -> none
    unnamed x34 -> x5, local copies, waits for them, and re-layouts: 46.4 us -> 4.6 us
    dot_general x8 -> x0, matrix products: 29.2 us -> none  [the longest x1 7.58 us: shards(): jnp.einsum('bhqk,bkhd->bqhd', probs, value_heads, preferred_element_type=...]
    convert_element_type x1 -> x0, local copies, waits for them, and re-layouts: 25 us -> none  [shards(): input_part.astype(jnp.bfloat16)]
  transfers between devices with their start and end apart: 9 -> 0, of which waited for: 5 -> 0; matrix products, arithmetic and copies ran while one was open for 31% -> 0% of each run, Pallas kernels for 0% -> 0%
where the time goes in v2:
time: 92.7 us; the launch traced here: 92.5 us
  Pallas kernels  87.3 us (94%)
  local copies, waits for them, and re-layouts  4.6 us (5%)
    pallas_call x1, Pallas kernels, shards(): pl.pallas_call(kernel, out_shape=(jax.ShapeDtypeStruct((T, C), BF16), jax...  87.3 us
    unnamed x5, local copies, waits for them, and re-layouts  4.6 us

profile of v2, /device:TPU:2, one launch (start us, length us, event | category | flops | bytes accessed | tf_op | source)
XLA Modules:
  0.0 92.5 jit_solution(4555498582392535892)
XLA Ops:
  0.6 87.3 %routed_attention.1 = (bf16[256,512]{1,0:T(8,128)(2,1)}, bf16[256,1024]{1,0:T(8,128)(2,1)}, f32[2,256,512]{2,1,0:T(8,128)}) custom-call(bf16[1,256,4096]{2,1,0:T(8,128)(2,1)} %act.1, s32[1,256]{1,0:T(1,128)} %mod.1, bf16[1,256,512]{2,1,0:T(8,128)(2,1)} %qin.1, bf16[1,256,512]{2,1,0:T(8,128)(2,1)} %kin.1, bf16[2,256,512]{2,1,0:T(8,128)(2,1)} %win.1, ...), custom_call_target="tpu_custom_call" | custom-call | tf_op jit(solution)/shard_map/routed_attention/pallas_call | solution.py:461
  87.9 0.0 copy-start
  87.9 1.8 %copy.12 = bf16[1,256,512]{2,1,0:T(8,128)(2,1)} copy(bf16[1,256,512]{2,1,0:T(8,128)(2,1)} %bitcast.3) | data formatting | bytes 524288
  89.7 1.9 %copy.13 = bf16[1,256,1024]{2,1,0:T(8,128)(2,1)} copy(bf16[1,256,1024]{2,1,0:T(8,128)(2,1)} %bitcast.2) | data formatting | bytes 1048576
  91.5 0.0 copy-done
  91.5 1.0 %copy.14 = f32[2,256,512]{2,1,0:T(8,128)} copy(f32[2,256,512]{2,1,0:T(8,128)S(1)} %copy-done) | data formatting | bytes 2097152
Async XLA Ops:
  87.9 3.6 %copy-start = (f32[2,256,512]{2,1,0:T(8,128)S(1)}, f32[2,256,512]{2,1,0:T(8,128)}, u32[]{:S(2)}) copy-start(f32[2,256,512]{2,1,0:T(8,128)} %get-tuple-element.14) | copy-start | bytes 3145732

commit v3 on v0

v3 whole, which is shorter than its diff:
```python
import functools

import jax
import jax.numpy as jnp
from jax import lax
from jax.experimental import pallas as pl
from jax.experimental.pallas import tpu as pltpu
from jax.sharding import PartitionSpec as P

HD = 128
BLOCK = 128
EXP2_SCALE = HD ** (-0.5) * 1.4426950408889634
NEG = -1e30
MESH = pl.DeviceIdType.MESH
F32 = jnp.float32
BF16 = jnp.bfloat16

T = 256
C = 512
F = 1024
FB = 256
NH = C // HD
CH = C // 2


def dot(a, b, ca, cb):
    return lax.dot_general(a, b, (((ca,), (cb,)), ((), ())), preferred_element_type=F32)


def wrap(v):
    return lax.rem(v + 4, 4)


def kernel(
    act, mod, qin, kin, win, gin,
    ctx_out, ig_out, wg_out,
    mod_v, mg, ag, wg, qg, gg, kg, vg, dv,
    pt, st, fa, gs,
    d_part, d_in, d_own,
    v_part, v_in, v_own,
    c_part, c_in, c_own, co,
    i_part, i_in, i_own, igs, igo,
    w_other, w_recv, w_own, w_mine, w_part, w_in, wo,
    loc_sem, sems,
):
    c = lax.axis_index("dp")
    s = lax.axis_index("sect")
    z = lax.axis_index("head")
    y = s // 4
    x = lax.rem(s, 4)

    def on_x(d):
        return (c, y * 4 + wrap(x + d), z)

    def on_y(d):
        return (c, wrap(y + d) * 4 + x, z)

    def on_z(d):
        return (c, s, wrap(z + d))

    partner = (1 - c, s, z)
    copies, arrived = [], set()

    def remote(src, dst, dev):
        n = len(copies)
        copy = pltpu.make_async_remote_copy(
            src_ref=src, dst_ref=dst, send_sem=sems.at[0, n], recv_sem=sems.at[1, n],
            device_id=dev, device_id_type=MESH,
        )
        copies.append(copy)
        copy.start()
        return copy

    def need(*some):
        for copy in some:
            if id(copy) not in arrived:
                arrived.add(id(copy))
                copy.wait_recv()

    class Gather:
        def __init__(self, on, slot, own=None, fixed=False, after=()):
            self.on, self.slot, self.fixed, self.after = on, slot, fixed, after
            self.own = own or (lambda part: slot(0, part))
            self.far = []

        def there(self, d, part, step):
            return self.slot(d, part) if self.fixed else self.slot((d + step) % 4, part)

        def start(self):
            need(*self.after)
            a_up = remote(self.own(0), self.there(0, 0, 1), self.on(1))
            b_dn = remote(self.own(1), self.there(0, 1, -1), self.on(-1))
            b_up = remote(self.own(1), self.there(0, 1, 1), self.on(1))
            a_dn = remote(self.own(0), self.there(0, 0, -1), self.on(-1))
            self.near_1, self.near_3 = (a_up, b_up), (b_dn, a_dn)

        def ra(self):
            need(self.near_1[0])
            self.far.append(remote(self.slot(1, 0), self.there(1, 0, 1), self.on(1)))

        def rb(self):
            need(self.near_3[0])
            self.far.append(remote(self.slot(3, 1), self.there(3, 1, -1), self.on(-1)))

        def finish(self):
            need(*self.near_1, *self.near_3, *self.far)

    def gather(on, buf, u, own=None):
        cols = pl.ds(u * CH, CH)
        return Gather(on, lambda d, part: buf.at[d, pl.ds(part * (T // 2), T // 2), cols], own)

    class Sum:
        def __init__(self, on, part, inbox, own, half, cols):
            self.on, self.own, self.half, self.cols = on, own, half, pl.ds(*cols)
            self.part = lambda e, n: part.at[e - 1, pl.ds(n * half, half), self.cols]
            self.inbox = lambda n: inbox.at[n, :, self.cols]

        def far(self):
            self.f_up = remote(self.part(2, 0), self.inbox(0), self.on(1))
            self.f_dn = remote(self.part(2, 1), self.inbox(1), self.on(-1))

        def near_up(self):
            self.n_up = remote(self.part(1, 1), self.inbox(2), self.on(1))

        def near_dn(self):
            self.n_dn = remote(self.part(3, 0), self.inbox(3), self.on(-1))

        def ra(self):
            need(self.f_up)
            here = self.part(1, 0)
            here[...] = (here[...].astype(F32) + self.inbox(0)[...].astype(F32)).astype(BF16)
            self.s_up = remote(here, self.inbox(4), self.on(1))

        def rb(self):
            need(self.f_dn)
            here = self.part(3, 1)
            here[...] = (here[...].astype(F32) + self.inbox(1)[...].astype(F32)).astype(BF16)
            self.s_dn = remote(here, self.inbox(5), self.on(-1))

        def finish(self, out):
            need(self.n_up, self.n_dn, self.s_up, self.s_dn)
            for n, sources in enumerate(((4, 3), (2, 5))):
                rows = pl.ds(n * self.half, self.half)
                total = self.own[rows, self.cols]
                for source in sources:
                    total = total + self.inbox(source)[...].astype(F32)
                out[rows, self.cols] = total.astype(out.dtype)

    local = [
        pltpu.make_async_copy(mod, mod_v, loc_sem.at[0]),
        *(
            pltpu.make_async_copy(
                act.at[0, :, pl.ds(pl.multiple_of(n * F + x * FB, FB), FB)], ag.at[0, :, pl.ds(n * FB, FB)],
                loc_sem.at[7 + n],
            )
            for n in range(4)
        ),
        pltpu.make_async_copy(qin.at[0], qg.at[0], loc_sem.at[2]),
        pltpu.make_async_copy(kin.at[0], kg.at[0], loc_sem.at[3]),
        pltpu.make_async_copy(gin.at[0], gg.at[0], loc_sem.at[4]),
        pltpu.make_async_copy(win.at[0], wg.at[0, y], loc_sem.at[5]),
        pltpu.make_async_copy(win.at[1], wg.at[1, y], loc_sem.at[6]),
    ]
    for copy in local:
        copy.start()

    barrier = pltpu.get_barrier_semaphore()
    for d in (1, 2, 3):
        for dev in (on_x(d), on_y(d), on_z(d)):
            pl.semaphore_signal(barrier, inc=1, device_id=dev, device_id_type=MESH)
    pl.semaphore_signal(barrier, inc=1, device_id=partner, device_id_type=MESH)
    pl.semaphore_wait(barrier, 10)

    def hbm_half(ref, u):
        return lambda part: ref.at[0, pl.ds(part * (T // 2), T // 2), pl.ds(u * CH, CH)]

    q_all, k_all, g_all, d_all, v_all = (
        [gather(on, buf, u, None if src is None else hbm_half(src, u)) for u in range(2)]
        for on, buf, src in (
            (on_x, qg, qin), (on_y, kg, kin), (on_x, gg, gin), (on_x, dv, None), (on_y, vg, None)
        )
    )
    d_sum, v_sum, c_sum = (
        [Sum(on, part, inbox, own, T // 2, (u * CH, CH)) for u in range(2)]
        for on, part, inbox, own in (
            (on_y, d_part, d_in, d_own), (on_x, v_part, v_in, v_own), (on_x, c_part, c_in, c_own)
        )
    )
    i_sum = [Sum(on_z, i_part.at[b], i_in.at[b], i_own.at[b], T // 2, (0, FB)) for b in range(4)]
    w_sum = [Sum(on_y, w_part, w_in, w_mine, FB // 2, (u * CH, CH)) for u in range(2)]
    w_all = Gather(
        on_y, lambda d, part: wg.at[c, wrap(y - d), pl.ds(part * (FB // 2), FB // 2)],
        lambda part: win.at[c, pl.ds(part * (FB // 2), FB // 2)], fixed=True,
    )

    quarter = pl.ds(pl.multiple_of(z * (T // 4), T // 4), T // 4)
    a_x = []

    def spread():
        for d in (1, 3, 2):
            for n in range(4):
                theirs = pl.ds(pl.multiple_of(n * F + wrap(x + d) * FB, FB), FB)
                a_x.append(
                    remote(act.at[0, quarter, theirs], ag.at[d, quarter, pl.ds(n * FB, FB)], on_x(d))
                )

    def z_slot(d, part):
        first = pl.multiple_of(wrap(z - d) * (T // 4) + part * (T // 8), T // 8)
        return ag.at[pl.ds(1, 3), pl.ds(first, T // 8)]

    a_all = Gather(on_z, z_slot, fixed=True, after=a_x)

    ahead = lax.broadcasted_iota(jnp.int32, (T, T), 1) - lax.broadcasted_iota(jnp.int32, (T, T), 0)

    shut = [jnp.where(y >= b, 0.0, NEG) for b in range(4)]

    def scores(u, first, last):
        k_all[u].finish()
        q_all[u].finish()

        def block(a, _):
            p = wrap(x - a)
            cols = pl.ds(pl.multiple_of(a * T, T), T)
            for n in range(2):
                h = 2 * u + n
                hs = slice(h * HD, (h + 1) * HD)
                parts, tops = [], []
                for b in range(4):
                    sc = dot(kg[b, :, hs], qg[a, :, hs], 1, 1)
                    if b == 0:
                        sc = jnp.where(ahead >= (x - p) * T, sc, NEG)
                    parts.append(sc)
                    tops.append(jnp.max(sc, axis=0, keepdims=True) + shut[b])
                top = jnp.maximum(functools.reduce(jnp.maximum, tops), 0.1 * NEG)
                total = jnp.zeros((1, T), F32)
                for b in range(4):
                    pw = jnp.exp2(parts[b] * EXP2_SCALE - (top - shut[b]) * EXP2_SCALE)
                    total = total + jnp.sum(pw, axis=0, keepdims=True)
                    pt[h, b * T:(b + 1) * T, cols] = pw.astype(BF16)
                for m in range(2):
                    st[u, 0, p, 2 * n + m:2 * n + m + 1] = top[:, m * BLOCK:(m + 1) * BLOCK]
                    st[u, 0, p, 4 + 2 * n + m:5 + 2 * n + m] = total[:, m * BLOCK:(m + 1) * BLOCK]
            return 0

        lax.fori_loop(first, last, block, 0)

    st_x = [[], []]

    def send_stats(u):
        for d in (1, 3, 2):
            st_x[u].append(remote(st.at[u, 0], st.at[u, d], on_x(d)))

    def factor(a, h):
        return jnp.concatenate([fa[a, h]] * (HD // 8), axis=0)

    def scale(u):
        need(*st_x[u])
        g_all[u].finish()
        for a in range(4):
            p = wrap(x - a)
            tops = [st[u, d, p, 0:4] for d in range(4)]
            top = functools.reduce(jnp.maximum, tops)
            total = jnp.zeros_like(top)
            for d in range(4):
                total = total + st[u, d, p, 4:8] * jnp.exp2((tops[d] - top) * EXP2_SCALE)
            each = jnp.exp2((tops[0] - top) * EXP2_SCALE) / total
            for n in range(2):
                for m in range(2):
                    row = each[2 * n + m:2 * n + m + 1]
                    fa[a, 2 * u + n, :, m * BLOCK:(m + 1) * BLOCK] = jnp.broadcast_to(row, (8, BLOCK))
        for h in (2 * u, 2 * u + 1):
            hs = slice(h * HD, (h + 1) * HD)
            for a in range(4):
                wide = factor(a, h).T
                gs[a * T:(a + 1) * T, hs] = (gg[a, :, hs].astype(F32) * wide).astype(BF16)

    def d_block(u, e):
        b = (4 - e) % 4
        for h in (2 * u, 2 * u + 1):
            hs = slice(h * HD, (h + 1) * HD)
            part = dot(pt[h, b * T:(b + 1) * T, :], gs[:, hs], 1, 0)
            if e:
                d_part[e - 1, :, hs] = part.astype(BF16)
            else:
                d_own[:, hs] = part

    m_x, w_c = {}, {}

    def image_rows(b, width):
        if b:
            need(m_x[b])
        parts = []
        for n in range(T // BLOCK):
            tile = mg[b, :, n * BLOCK:(n + 1) * BLOCK]
            tile = jnp.concatenate([tile] * (width // BLOCK), axis=1)
            parts += [tile] * (BLOCK // 8)
        return jnp.concatenate(parts, axis=0) == 1

    def i_block(b, e):
        need(*w_c.values())
        for u in range(2):
            need(*((), d_all[u].near_1, d_all[u].far, d_all[u].near_3)[b])
        n = wrap(z + e)
        rows = dv[b]
        text = dot(rows, wg[0, n], 1, 1)
        image = dot(rows, wg[1, n], 1, 1)
        part = jnp.where(image_rows(b, FB), image, text)
        if e:
            i_part[b, e - 1] = part.astype(BF16)
        else:
            i_own[b] = part

    i_x = []

    def i_done(b):
        cols = pl.ds(pl.multiple_of(x * FB, FB), FB)
        if b:
            i_sum[b].finish(igs.at[b])
            i_x.append(remote(igs.at[b], igo.at[:, cols], on_x(-b)))
        else:
            i_sum[0].finish(igo.at[:, cols])

    def v_block(e):
        need(*w_c.values())
        a_all.finish()
        b = (4 - e) % 4
        rows = ag[b]
        text = dot(rows, wg[0].reshape(F, C), 1, 0)
        image = dot(rows, wg[1].reshape(F, C), 1, 0)
        part = jnp.where(image_rows(b, C), image, text)
        if e:
            v_part[e - 1] = part.astype(BF16)
        else:
            v_own[...] = part

    def update(kind, u):
        a_all.finish()
        d_all[u].finish()
        cols = slice(u * CH, (u + 1) * CH)
        masked = [
            jnp.where(image_rows(b, CH) == (kind == 1), dv[b, :, cols].astype(F32), 0.0).astype(BF16)
            for b in range(4)
        ]
        return dot(ag[...].reshape(4 * T, F), jnp.concatenate(masked, axis=0), 0, 0)

    def c_block(u, e):
        v_all[u].finish()
        a = (4 - e) % 4
        for h in (2 * u, 2 * u + 1):
            hs = slice(h * HD, (h + 1) * HD)
            values = vg[:, :, hs].reshape(4 * T, HD)
            part = dot(values, pt[h, :, a * T:(a + 1) * T], 0, 0)
            part = (part * factor(a, h)).T
            if e:
                c_part[e - 1, :, hs] = part.astype(BF16)
            else:
                c_own[:, hs] = part

    def d_done(u):
        d_sum[u].finish(dv.at[0])

    def v_done(u):
        v_sum[u].finish(vg.at[0])

    def c_done(u):
        c_sum[u].finish(co)

    def hand(d):
        need(*(w_all.near_1, w_all.far, w_all.near_3)[d - 1])
        block = wg.at[c, wrap(y - d)]
        w_c[d] = remote(block, block, partner)

    w_x, w_back = {}, []

    def w_other_kind(u):
        w_other[u] = update(1 - c, u).astype(BF16)
        w_x[u] = remote(w_other.at[u], w_recv.at[u], partner)

    def w_own_kind(u):
        w_own[u] = update(c, u)

    def w_add(u):
        need(w_x[u])
        cols = slice(u * CH, (u + 1) * CH)
        for e in range(4):
            rows = pl.ds(pl.multiple_of(wrap(y + e) * FB, FB), FB)
            summed = w_own[u, rows, :] + w_recv[u, rows, :].astype(F32)
            if e:
                w_part[e - 1, :, cols] = summed.astype(BF16)
            else:
                w_mine[:, cols] = summed

    def w_done(u):
        w_sum[u].finish(wo.at[c])
        block = wo.at[c, :, pl.ds(u * CH, CH)]
        w_back.append(remote(block, block, partner))

    spread()
    k_all[0].start()
    q_all[0].start()
    for copy in local:
        copy.wait()
    mg[0] = jnp.broadcast_to(mod_v[...], (8, T))
    for d in (1, 2, 3):
        m_x[d] = remote(mg.at[0], mg.at[d], on_x(d))
    k_all[0].ra()
    k_all[0].rb()
    k_all[1].start()
    k_all[1].ra()
    k_all[1].rb()
    w_all.start()
    a_all.start()
    q_all[0].ra()
    q_all[0].rb()
    q_all[1].start()
    scores(0, 0, 2)
    q_all[1].ra()
    q_all[1].rb()
    g_all[0].start()
    scores(0, 2, 4)
    send_stats(0)
    w_all.ra()
    w_all.rb()
    a_all.ra()
    a_all.rb()
    hand(1)
    hand(3)
    scores(1, 0, 2)
    g_all[0].ra()
    g_all[0].rb()
    g_all[1].start()
    scores(1, 2, 4)
    send_stats(1)
    hand(2)
    scale(0)
    d_block(0, 1)
    d_sum[0].near_up()
    v_block(2)
    g_all[1].ra()
    g_all[1].rb()
    v_sum[0].far()
    v_block(1)
    v_sum[0].near_up()
    v_block(3)
    v_sum[0].near_dn()
    v_block(0)
    v_sum[1].far()
    v_sum[1].near_dn()
    v_sum[1].near_up()
    d_block(0, 2)
    d_sum[0].far()
    d_block(0, 3)
    d_sum[0].near_dn()
    d_block(0, 0)
    scale(1)
    d_block(1, 1)
    d_sum[1].near_up()
    d_block(1, 2)
    d_sum[1].far()
    v_sum[0].ra()
    v_sum[0].rb()
    d_block(1, 3)
    d_sum[1].near_dn()
    d_sum[0].ra()
    d_sum[0].rb()
    d_block(1, 0)
    v_sum[1].ra()
    v_sum[1].rb()
    d_sum[1].rb()
    d_sum[1].ra()
    v_done(0)
    v_all[0].start()
    d_done(0)
    d_all[0].start()
    v_done(1)
    v_all[1].start()
    d_done(1)
    d_all[1].start()
    i_block(0, 2)
    i_sum[0].far()
    i_block(0, 1)
    i_sum[0].near_up()
    i_block(0, 3)
    i_sum[0].near_dn()
    i_block(0, 0)
    v_all[0].ra()
    v_all[0].rb()
    d_all[0].ra()
    d_all[0].rb()
    i_sum[0].ra()
    v_all[1].ra()
    v_all[1].rb()
    i_sum[0].rb()
    d_all[1].ra()
    d_all[1].rb()
    i_block(1, 2)
    i_sum[1].far()
    i_block(1, 1)
    i_sum[1].near_up()
    i_block(1, 3)
    i_sum[1].near_dn()
    i_block(1, 0)
    i_block(3, 2)
    i_sum[3].far()
    i_block(3, 1)
    i_sum[3].near_up()
    i_block(3, 3)
    i_sum[3].near_dn()
    i_done(0)
    i_block(3, 0)
    w_other_kind(0)
    i_block(2, 2)
    i_sum[2].far()
    i_block(2, 1)
    i_sum[1].ra()
    i_sum[1].rb()
    i_sum[2].near_up()
    i_block(2, 3)
    i_sum[2].near_dn()
    i_block(2, 0)
    w_own_kind(0)
    c_block(0, 2)
    c_sum[0].far()
    c_block(0, 1)
    c_sum[0].near_up()
    c_block(0, 3)
    c_sum[0].near_dn()
    c_block(0, 0)
    w_other_kind(1)
    i_sum[3].ra()
    i_sum[3].rb()
    w_add(0)
    w_own_kind(1)
    c_block(1, 2)
    c_sum[1].far()
    w_sum[0].far()
    w_sum[0].near_dn()
    w_sum[0].near_up()
    c_block(1, 1)
    c_sum[1].near_up()
    c_sum[0].ra()
    c_sum[0].rb()
    c_block(1, 3)
    c_sum[1].near_dn()
    c_block(1, 0)
    i_sum[2].ra()
    i_sum[2].rb()
    w_add(1)
    w_sum[1].far()
    i_done(1)
    w_sum[1].near_dn()
    w_sum[1].near_up()
    c_sum[1].ra()
    c_sum[1].rb()
    w_sum[0].ra()
    w_sum[0].rb()
    i_done(3)
    c_done(0)
    w_sum[1].ra()
    w_sum[1].rb()
    i_done(2)
    w_done(0)
    c_done(1)
    w_done(1)

    need(*i_x)
    out_i = pltpu.make_async_copy(igo, ig_out, loc_sem.at[1])
    out_i.start()
    need(*w_back)
    out_w = pltpu.make_async_copy(wo, wg_out, loc_sem.at[2])
    out_w.start()
    out_c = pltpu.make_async_copy(co, ctx_out, loc_sem.at[0])
    out_c.start()
    need(*copies)
    for copy in copies:
        copy.wait_send()
    out_c.wait()
    out_i.wait()
    out_w.wait()


def shards(activations, modality, query_rows, key_rows, value_weight, context_grad):
    vm = lambda shape, dtype=BF16: pltpu.VMEM(shape, dtype)
    dma = lambda *shape: pltpu.SemaphoreType.DMA(shape)
    any_spec = pl.BlockSpec(memory_space=pl.ANY)
    ring_sum = lambda rows, cols: [vm((3, rows, cols)), vm((6, rows // 2, cols)), vm((rows, cols), F32)]
    ctx, ig, wgrad = pl.pallas_call(
        kernel,
        out_shape=(
            jax.ShapeDtypeStruct((T, C), BF16),
            jax.ShapeDtypeStruct((T, F), BF16),
            jax.ShapeDtypeStruct((2, T, C), F32),
        ),
        in_specs=[any_spec] * 6,
        out_specs=(any_spec,) * 3,
        scratch_shapes=[
            vm((1, T), jnp.int32), vm((4, 8, T), jnp.int32), vm((4, T, F)), vm((2, 4, FB, C)),
            vm((4, T, C)), vm((4, T, C)), vm((4, T, C)), vm((4, T, C)), vm((4, T, C)),
            vm((NH, 4 * T, 4 * T)), vm((2, 4, 4, 8, BLOCK), F32), vm((4, NH, 8, T), F32), vm((4 * T, C)),
            *ring_sum(T, C), *ring_sum(T, C), *ring_sum(T, C), vm((T, C)),
            vm((4, 3, T, FB)), vm((4, 6, T // 2, FB)), vm((4, T, FB), F32), vm((4, T, FB)), vm((T, F)),
            vm((2, F, CH)), vm((2, F, CH)), vm((2, F, CH), F32), vm((FB, C), F32), vm((3, FB, C)), vm((6, FB // 2, C)), vm((2, FB, C), F32),
            dma(11), dma(2, 192),
        ],
        compiler_params=pltpu.CompilerParams(
            collective_id=0, has_side_effects=True, vmem_limit_bytes=60 * 2**20
        ),
        name="routed_attention",
    )(activations, modality, query_rows, key_rows, value_weight, context_grad)
    return tuple(hand_out(ctx[None], ig[None], wgrad))


def hand_out_kernel(*refs):
    sem = refs[-1]
    moves = []
    for src, buf, dst in zip(refs[:3], refs[6:9], refs[3:6]):
        for n in range(src.shape[0]):
            for m in range(2):
                rows = pl.ds(m * 128, 128)
                k = len(moves)
                moves.append((
                    pltpu.make_async_copy(src.at[n, rows], buf.at[n, rows], sem.at[0, k]),
                    pltpu.make_async_copy(buf.at[n, rows], dst.at[n, rows], sem.at[1, k]),
                ))
    for come, _ in moves:
        come.start()
    for come, go in moves:
        come.wait()
        go.start()
    for _, go in moves:
        go.wait()


def hand_out(*arrays):
    any_spec = pl.BlockSpec(memory_space=pl.ANY)
    return pl.pallas_call(
        hand_out_kernel,
        out_shape=tuple(jax.ShapeDtypeStruct(a.shape, a.dtype) for a in arrays),
        in_specs=[any_spec] * 3,
        out_specs=(any_spec,) * 3,
        scratch_shapes=[*(pltpu.VMEM(a.shape, a.dtype) for a in arrays), pltpu.SemaphoreType.DMA((2, 8))],
        name="hand_out",
    )(*arrays)


def solution(mesh):
    return jax.shard_map(
        shards,
        mesh=mesh,
        in_specs=(
            P("dp", "sect", None),
            P("dp", "sect"),
            P("dp", "sect", "head"),
            P("dp", "sect", "head"),
            P(None, "sect", "head"),
            P("dp", "sect", "head"),
        ),
        out_specs=(P("dp", "sect", "head"), P("dp", "sect", "head"), P(None, "sect", "head")),
        check_vma=False,
    )
```

time: 494 us -> 86.2 us (0.17)
  waiting for transfers between devices: 240 us -> 0 us
  local copies, waits for them, and re-layouts: 84.9 us -> 0 us
  Pallas kernels: 0 us -> 83.7 us
  other arithmetic: 54.7 us -> 0 us
  blocking collectives: 43.7 us -> 0 us
  matrix products: 40.7 us -> 0 us
  between operations: 15 us -> 0.82 us
  starting transfers between devices: 13.1 us -> 0 us
    all_gather x4 -> x0, waiting for transfers between devices: 129 us -> none  [the longest x1 70.3 us: shards(): lax.all_gather(value_weight, 'sect', axis=1, tiled=True)]
    reduce_scatter x2 -> x0, waiting for transfers between devices: 105 us -> none  [the longest x1 84.1 us: shards(): lax.psum_scatter(term.reshape(row_count * lax.axis_size('sect'), seq_coun...]
    pallas_call x0 -> x2, Pallas kernels: none -> 83.7 us  [the longest x1 81.3 us: shards(): pl.pallas_call(kernel, out_shape=(jax.ShapeDtypeStruct((T, C), BF16), jax...]
    unnamed x34 -> x0, local copies, waits for them, and re-layouts: 46.4 us -> none
    unnamed x2 -> x0, other arithmetic: 44.5 us -> none
    unnamed x1 -> x0, blocking collectives: 43.7 us -> none
    dot_general x8 -> x0, matrix products: 29.2 us -> none  [the longest x1 7.58 us: shards(): jnp.einsum('bhqk,bkhd->bqhd', probs, value_heads, preferred_element_type=...]
    convert_element_type x1 -> x0, local copies, waits for them, and re-layouts: 25 us -> none  [shards(): input_part.astype(jnp.bfloat16)]
  transfers between devices with their start and end apart: 9 -> 0, of which waited for: 5 -> 0; matrix products, arithmetic and copies ran while one was open for 31% -> 0% of each run, Pallas kernels for 0% -> 0%
where the time goes in v3:
time: 86.2 us; the launch traced here: 84.5 us
  Pallas kernels  83.7 us (97%)
    pallas_call x1, Pallas kernels, shards(): pl.pallas_call(kernel, out_shape=(jax.ShapeDtypeStruct((T, C), BF16), jax...  81.3 us
    pallas_call x1, Pallas kernels, hand_out(): pl.pallas_call(hand_out_kernel, out_shape=tuple((jax.ShapeDtypeStruct(a.s...  2.36 us

profile of v3, /device:TPU:2, one launch (start us, length us, event | category | flops | bytes accessed | tf_op | source)
XLA Modules:
  0.0 84.5 jit_solution(4300235844358413598)
XLA Ops:
  0.6 81.3 %routed_attention.1 = (bf16[256,512]{1,0:T(8,128)(2,1)}, bf16[256,1024]{1,0:T(8,128)(2,1)}, f32[2,256,512]{2,1,0:T(8,128)}) custom-call(bf16[1,256,4096]{2,1,0:T(8,128)(2,1)} %act.1, s32[1,256]{1,0:T(1,128)} %mod.1, bf16[1,256,512]{2,1,0:T(8,128)(2,1)} %qin.1, bf16[1,256,512]{2,1,0:T(8,128)(2,1)} %kin.1, bf16[2,256,512]{2,1,0:T(8,128)(2,1)} %win.1, ...), custom_call_target="tpu_custom_call" | custom-call | tf_op jit(solution)/shard_map/routed_attention/pallas_call | solution.py:587
  82.0 2.4 %hand_out.1 = (bf16[1,256,512]{2,1,0:T(8,128)(2,1)}, bf16[1,256,1024]{2,1,0:T(8,128)(2,1)}, f32[2,256,512]{2,1,0:T(8,128)}) custom-call(bf16[1,256,512]{2,1,0:T(8,128)(2,1)} %bitcast.3, bf16[1,256,1024]{2,1,0:T(8,128)(2,1)} %bitcast.2, f32[2,256,512]{2,1,0:T(8,128)} %get-tuple-element.8.refs_2_), custom_call_target="tpu_custom_call" | custom-call | tf_op jit(solution)/shard_map/hand_out/pallas_call | solution.py:636

commit v4 on v3

--- a/solution.py
+++ b/solution.py
@@ -299,7 +299,8 @@
     def i_block(b, e):
         need(*w_c.values())
         for u in range(2):
-            need(*((), d_all[u].near_1, d_all[u].far, d_all[u].near_3)[b])
+            if b:
+                need(*(d_all[u].near_1, d_all[u].far, d_all[u].near_3)[b - 1])
         n = wrap(z + e)
         rows = dv[b]
         text = dot(rows, wg[0, n], 1, 1)
@@ -395,24 +396,24 @@
         block = wo.at[c, :, pl.ds(u * CH, CH)]
         w_back.append(remote(block, block, partner))
 
+    q_all[0].start()
+    k_all[0].start()
     spread()
-    k_all[0].start()
-    q_all[0].start()
     for copy in local:
         copy.wait()
     mg[0] = jnp.broadcast_to(mod_v[...], (8, T))
     for d in (1, 2, 3):
         m_x[d] = remote(mg.at[0], mg.at[d], on_x(d))
+    q_all[0].ra()
+    q_all[0].rb()
     k_all[0].ra()
+    q_all[1].start()
     k_all[0].rb()
     k_all[1].start()
     k_all[1].ra()
     k_all[1].rb()
     w_all.start()
     a_all.start()
-    q_all[0].ra()
-    q_all[0].rb()
-    q_all[1].start()
     scores(0, 0, 2)
     q_all[1].ra()
     q_all[1].rb()
@@ -421,55 +422,53 @@
     send_stats(0)
     w_all.ra()
     w_all.rb()
-    a_all.ra()
+    scores(1, 0, 2)
+    g_all[0].rb()
+    g_all[0].ra()
+    g_all[1].start()
     a_all.rb()
     hand(1)
     hand(3)
-    scores(1, 0, 2)
-    g_all[0].ra()
-    g_all[0].rb()
-    g_all[1].start()
+    a_all.ra()
     scores(1, 2, 4)
     send_stats(1)
     hand(2)
     scale(0)
     d_block(0, 1)
+    d_block(0, 2)
+    g_all[1].rb()
+    g_all[1].ra()
+    d_block(0, 0)
+    d_sum[0].far()
     d_sum[0].near_up()
+    d_block(0, 3)
+    d_sum[0].near_dn()
     v_block(2)
-    g_all[1].ra()
-    g_all[1].rb()
+    v_sum[1].far()
     v_sum[0].far()
-    v_block(1)
-    v_sum[0].near_up()
     v_block(3)
     v_sum[0].near_dn()
-    v_block(0)
-    v_sum[1].far()
-    v_sum[1].near_dn()
-    v_sum[1].near_up()
-    d_block(0, 2)
-    d_sum[0].far()
-    d_block(0, 3)
-    d_sum[0].near_dn()
-    d_block(0, 0)
     scale(1)
+    d_block(1, 2)
+    d_sum[1].far()
     d_block(1, 1)
     d_sum[1].near_up()
-    d_block(1, 2)
-    d_sum[1].far()
+    d_block(1, 3)
+    d_sum[1].near_dn()
+    v_block(1)
+    v_sum[1].near_up()
+    v_block(0)
+    v_sum[1].ra()
+    d_block(1, 0)
+    v_sum[1].near_dn()
+    v_sum[1].rb()
+    v_sum[0].near_up()
+    d_sum[0].rb()
+    d_sum[0].ra()
     v_sum[0].ra()
     v_sum[0].rb()
-    d_block(1, 3)
-    d_sum[1].near_dn()
-    d_sum[0].ra()
-    d_sum[0].rb()
-    d_block(1, 0)
-    v_sum[1].ra()
-    v_sum[1].rb()
+    d_sum[1].ra()
     d_sum[1].rb()
-    d_sum[1].ra()
-    v_done(0)
-    v_all[0].start()
     d_done(0)
     d_all[0].start()
     v_done(1)
@@ -480,87 +479,89 @@
     i_sum[0].far()
     i_block(0, 1)
     i_sum[0].near_up()
+    v_done(0)
+    v_all[0].start()
     i_block(0, 3)
     i_sum[0].near_dn()
     i_block(0, 0)
-    v_all[0].ra()
-    v_all[0].rb()
     d_all[0].ra()
     d_all[0].rb()
-    i_sum[0].ra()
     v_all[1].ra()
     v_all[1].rb()
+    i_sum[0].ra()
     i_sum[0].rb()
     d_all[1].ra()
     d_all[1].rb()
-    i_block(1, 2)
-    i_sum[1].far()
-    i_block(1, 1)
-    i_sum[1].near_up()
-    i_block(1, 3)
-    i_sum[1].near_dn()
-    i_block(1, 0)
-    i_block(3, 2)
-    i_sum[3].far()
+    v_all[0].ra()
+    v_all[0].rb()
     i_block(3, 1)
     i_sum[3].near_up()
     i_block(3, 3)
-    i_sum[3].near_dn()
-    i_done(0)
     i_block(3, 0)
+    i_block(1, 2)
+    i_sum[1].far()
+    i_block(1, 3)
+    i_block(1, 1)
+    i_sum[1].near_up()
+    i_sum[1].near_dn()
     w_other_kind(0)
+    w_own_kind(0)
     i_block(2, 2)
     i_sum[2].far()
     i_block(2, 1)
-    i_sum[1].ra()
-    i_sum[1].rb()
     i_sum[2].near_up()
     i_block(2, 3)
     i_sum[2].near_dn()
-    i_block(2, 0)
-    w_own_kind(0)
     c_block(0, 2)
     c_sum[0].far()
+    w_other_kind(1)
+    c_block(1, 3)
+    c_sum[1].near_dn()
+    i_sum[1].ra()
+    c_block(1, 2)
+    c_sum[1].far()
+    c_block(1, 0)
+    i_block(3, 2)
+    i_sum[3].far()
+    w_add(0)
+    w_sum[0].far()
+    w_sum[0].near_dn()
+    w_sum[0].near_up()
     c_block(0, 1)
     c_sum[0].near_up()
     c_block(0, 3)
     c_sum[0].near_dn()
+    i_sum[3].near_dn()
     c_block(0, 0)
-    w_other_kind(1)
-    i_sum[3].ra()
-    i_sum[3].rb()
-    w_add(0)
+    i_sum[2].rb()
+    c_sum[0].ra()
+    c_sum[0].rb()
+    i_block(1, 0)
+    i_sum[2].ra()
+    i_done(0)
+    i_sum[1].rb()
     w_own_kind(1)
-    c_block(1, 2)
-    c_sum[1].far()
-    w_sum[0].far()
-    w_sum[0].near_dn()
-    w_sum[0].near_up()
+    w_add(1)
+    w_sum[1].near_dn()
+    w_sum[1].near_up()
+    w_sum[1].far()
+    i_block(2, 0)
     c_block(1, 1)
     c_sum[1].near_up()
-    c_sum[0].ra()
-    c_sum[0].rb()
-    c_block(1, 3)
-    c_sum[1].near_dn()
-    c_block(1, 0)
-    i_sum[2].ra()
-    i_sum[2].rb()
-    w_add(1)
-    w_sum[1].far()
-    i_done(1)
-    w_sum[1].near_dn()
-    w_sum[1].near_up()
     c_sum[1].ra()
+    w_sum[0].rb()
+    w_sum[0].ra()
+    i_sum[3].rb()
     c_sum[1].rb()
-    w_sum[0].ra()
-    w_sum[0].rb()
-    i_done(3)
+    i_sum[3].ra()
     c_done(0)
+    i_done(2)
     w_sum[1].ra()
     w_sum[1].rb()
-    i_done(2)
+    i_done(1)
+    c_done(1)
     w_done(0)
-    c_done(1)
+    i_done(3)
     w_done(1)
 
     need(*i_x)

time: 86.2 us -> 82.4 us (0.956)
  Pallas kernels: 83.7 us -> 80.5 us
    pallas_call x1, Pallas kernels: 81.3 us -> 78.1 us  [shards(): pl.pallas_call(kernel, out_shape=(jax.ShapeDtypeStruct((T, C), BF16), jax...]
where the time goes in v4:
time: 82.4 us; the launch traced here: 81.3 us
  Pallas kernels  80.5 us (98%)
    pallas_call x1, Pallas kernels, shards(): pl.pallas_call(kernel, out_shape=(jax.ShapeDtypeStruct((T, C), BF16), jax...  78.1 us
    pallas_call x1, Pallas kernels, hand_out(): pl.pallas_call(hand_out_kernel, out_shape=tuple((jax.ShapeDtypeStruct(a.s...  2.36 us

profile of v4, /device:TPU:2, one launch (start us, length us, event | category | flops | bytes accessed | tf_op | source)
XLA Modules:
  0.0 81.3 jit_solution(16632338461658690984)
XLA Ops:
  0.6 78.1 %routed_attention.1 = (bf16[256,512]{1,0:T(8,128)(2,1)}, bf16[256,1024]{1,0:T(8,128)(2,1)}, f32[2,256,512]{2,1,0:T(8,128)}) custom-call(bf16[1,256,4096]{2,1,0:T(8,128)(2,1)} %act.1, s32[1,256]{1,0:T(1,128)} %mod.1, bf16[1,256,512]{2,1,0:T(8,128)(2,1)} %qin.1, bf16[1,256,512]{2,1,0:T(8,128)(2,1)} %kin.1, bf16[2,256,512]{2,1,0:T(8,128)(2,1)} %win.1, ...), custom_call_target="tpu_custom_call" | custom-call | tf_op jit(solution)/shard_map/routed_attention/pallas_call | solution.py:588
  78.8 2.4 %hand_out.1 = (bf16[1,256,512]{2,1,0:T(8,128)(2,1)}, bf16[1,256,1024]{2,1,0:T(8,128)(2,1)}, f32[2,256,512]{2,1,0:T(8,128)}) custom-call(bf16[1,256,512]{2,1,0:T(8,128)(2,1)} %bitcast.3, bf16[1,256,1024]{2,1,0:T(8,128)(2,1)} %bitcast.2, f32[2,256,512]{2,1,0:T(8,128)} %get-tuple-element.8.refs_2_), custom_call_target="tpu_custom_call" | custom-call | tf_op jit(solution)/shard_map/hand_out/pallas_call | solution.py:637

commit v5 on v3

--- a/solution.py
+++ b/solution.py
@@ -299,7 +299,8 @@
     def i_block(b, e):
         need(*w_c.values())
         for u in range(2):
-            need(*((), d_all[u].near_1, d_all[u].far, d_all[u].near_3)[b])
+            if b:
+                need(*(d_all[u].near_1, d_all[u].far, d_all[u].near_3)[b - 1])
         n = wrap(z + e)
         rows = dv[b]
         text = dot(rows, wg[0, n], 1, 1)
@@ -310,13 +311,13 @@
         else:
             i_own[b] = part
 
-    i_x = []
+    i_x = {}
 
     def i_done(b):
         cols = pl.ds(pl.multiple_of(x * FB, FB), FB)
         if b:
             i_sum[b].finish(igs.at[b])
-            i_x.append(remote(igs.at[b], igo.at[:, cols], on_x(-b)))
+            i_x[b] = remote(igs.at[b], igo.at[:, cols], on_x(-b))
         else:
             i_sum[0].finish(igo.at[:, cols])
 
@@ -395,16 +396,16 @@
         block = wo.at[c, :, pl.ds(u * CH, CH)]
         w_back.append(remote(block, block, partner))
 
+    k_all[0].start()
     spread()
-    k_all[0].start()
     q_all[0].start()
+    k_all[0].ra()
+    k_all[0].rb()
     for copy in local:
         copy.wait()
     mg[0] = jnp.broadcast_to(mod_v[...], (8, T))
     for d in (1, 2, 3):
         m_x[d] = remote(mg.at[0], mg.at[d], on_x(d))
-    k_all[0].ra()
-    k_all[0].rb()
     k_all[1].start()
     k_all[1].ra()
     k_all[1].rb()
@@ -416,13 +417,13 @@
     scores(0, 0, 2)
     q_all[1].ra()
     q_all[1].rb()
+    w_all.ra()
+    w_all.rb()
     g_all[0].start()
     scores(0, 2, 4)
-    send_stats(0)
-    w_all.ra()
-    w_all.rb()
     a_all.ra()
     a_all.rb()
+    send_stats(0)
     hand(1)
     hand(3)
     scores(1, 0, 2)
@@ -430,153 +431,155 @@
     g_all[0].rb()
     g_all[1].start()
     scores(1, 2, 4)
+    hand(2)
     send_stats(1)
-    hand(2)
     scale(0)
+    d_block(0, 3)
+    d_block(0, 2)
+    g_all[1].ra()
+    g_all[1].rb()
+    d_block(0, 0)
+    d_sum[0].far()
+    d_sum[0].near_dn()
     d_block(0, 1)
     d_sum[0].near_up()
     v_block(2)
-    g_all[1].ra()
-    g_all[1].rb()
     v_sum[0].far()
+    v_sum[1].far()
     v_block(1)
     v_sum[0].near_up()
+    v_sum[1].near_up()
+    v_block(0)
     v_block(3)
     v_sum[0].near_dn()
-    v_block(0)
-    v_sum[1].far()
     v_sum[1].near_dn()
-    v_sum[1].near_up()
-    d_block(0, 2)
-    d_sum[0].far()
-    d_block(0, 3)
-    d_sum[0].near_dn()
-    d_block(0, 0)
     scale(1)
-    d_block(1, 1)
-    d_sum[1].near_up()
     d_block(1, 2)
     d_sum[1].far()
+    d_sum[0].ra()
     v_sum[0].ra()
     v_sum[0].rb()
+    d_sum[0].rb()
+    d_block(1, 1)
     d_block(1, 3)
     d_sum[1].near_dn()
-    d_sum[0].ra()
-    d_sum[0].rb()
     d_block(1, 0)
+    d_sum[1].near_up()
     v_sum[1].ra()
     v_sum[1].rb()
+    d_sum[1].ra()
     d_sum[1].rb()
-    d_sum[1].ra()
+    d_done(0)
+    d_all[0].start()
     v_done(0)
     v_all[0].start()
-    d_done(0)
-    d_all[0].start()
     v_done(1)
     v_all[1].start()
     d_done(1)
     d_all[1].start()
     i_block(0, 2)
     i_sum[0].far()
+    i_block(0, 0)
+    d_all[0].ra()
+    d_all[0].rb()
     i_block(0, 1)
     i_sum[0].near_up()
     i_block(0, 3)
     i_sum[0].near_dn()
-    i_block(0, 0)
     v_all[0].ra()
     v_all[0].rb()
-    d_all[0].ra()
-    d_all[0].rb()
+    d_all[1].ra()
+    d_all[1].rb()
     i_sum[0].ra()
+    i_sum[0].rb()
     v_all[1].ra()
     v_all[1].rb()
-    i_sum[0].rb()
-    d_all[1].ra()
-    d_all[1].rb()
+    i_block(1, 1)
+    i_sum[1].near_up()
+    i_block(3, 1)
+    i_block(3, 3)
+    i_sum[3].near_dn()
+    i_sum[3].near_up()
+    i_block(1, 0)
+    i_block(1, 3)
+    i_sum[1].near_dn()
+    i_block(3, 2)
+    w_other_kind(0)
+    c_block(0, 1)
+    c_block(0, 3)
+    c_sum[0].near_dn()
+    c_block(0, 2)
+    c_sum[0].far()
+    i_block(2, 2)
+    i_sum[2].far()
+    i_block(2, 0)
+    w_other_kind(1)
+    c_block(1, 0)
+    i_sum[3].far()
+    c_block(0, 0)
     i_block(1, 2)
     i_sum[1].far()
-    i_block(1, 1)
-    i_sum[1].near_up()
-    i_block(1, 3)
-    i_sum[1].near_dn()
-    i_block(1, 0)
-    i_block(3, 2)
-    i_sum[3].far()
-    i_block(3, 1)
-    i_sum[3].near_up()
-    i_block(3, 3)
-    i_sum[3].near_dn()
-    i_done(0)
-    i_block(3, 0)
-    w_other_kind(0)
-    i_block(2, 2)
-    i_sum[2].far()
-    i_block(2, 1)
-    i_sum[1].ra()
-    i_sum[1].rb()
-    i_sum[2].near_up()
+    c_sum[0].near_up()
     i_block(2, 3)
     i_sum[2].near_dn()
-    i_block(2, 0)
-    w_own_kind(0)
-    c_block(0, 2)
-    c_sum[0].far()
-    c_block(0, 1)
-    c_sum[0].near_up()
-    c_block(0, 3)
-    c_sum[0].near_dn()
-    c_block(0, 0)
-    w_other_kind(1)
-    i_sum[3].ra()
-    i_sum[3].rb()
-    w_add(0)
-    w_own_kind(1)
+    i_block(3, 0)
     c_block(1, 2)
     c_sum[1].far()
+    w_own_kind(0)
+    c_sum[0].ra()
+    w_add(0)
     w_sum[0].far()
     w_sum[0].near_dn()
     w_sum[0].near_up()
+    i_sum[2].rb()
+    i_block(2, 1)
+    i_sum[2].near_up()
+    i_sum[2].ra()
+    c_sum[0].rb()
+    i_done(0)
     c_block(1, 1)
+    i_sum[3].ra()
+    i_sum[3].rb()
     c_sum[1].near_up()
-    c_sum[0].ra()
-    c_sum[0].rb()
-    c_block(1, 3)
-    c_sum[1].near_dn()
-    c_block(1, 0)
-    i_sum[2].ra()
-    i_sum[2].rb()
+    w_own_kind(1)
     w_add(1)
     w_sum[1].far()
-    i_done(1)
     w_sum[1].near_dn()
     w_sum[1].near_up()
+    c_block(1, 3)
+    i_sum[1].ra()
+    i_sum[1].rb()
+    c_sum[1].near_dn()
+    c_sum[1].rb()
     c_sum[1].ra()
-    c_sum[1].rb()
     w_sum[0].ra()
     w_sum[0].rb()
-    i_done(3)
     c_done(0)
+    i_done(2)
     w_sum[1].ra()
     w_sum[1].rb()
-    i_done(2)
+    i_done(3)
+    c_done(1)
+    i_done(1)
     w_done(0)
-    c_done(1)
     w_done(1)
 
-    need(*i_x)
-    out_i = pltpu.make_async_copy(igo, ig_out, loc_sem.at[1])
-    out_i.start()
+    outs = [pltpu.make_async_copy(co, ctx_out, loc_sem.at[0])]
+    outs[0].start()
     need(*w_back)
-    out_w = pltpu.make_async_copy(wo, wg_out, loc_sem.at[2])
-    out_w.start()
-    out_c = pltpu.make_async_copy(co, ctx_out, loc_sem.at[0])
-    out_c.start()
+    outs.append(pltpu.make_async_copy(wo, wg_out, loc_sem.at[1]))
+    outs[1].start()
+    for b in (0, 1, 3, 2):
+        if b:
+            need(i_x[b])
+        cols = pl.ds(pl.multiple_of(wrap(x + b) * FB, FB), FB)
+        outs.append(pltpu.make_async_copy(igo.at[:, cols], ig_out.at[:, cols], loc_sem.at[2 + b]))
+        outs[-1].start()
     need(*copies)
     for copy in copies:
         copy.wait_send()
-    out_c.wait()
-    out_i.wait()
-    out_w.wait()
+    for copy in outs:
+        copy.wait()
 
 
 def shards(activations, modality, query_rows, key_rows, value_weight, context_grad):

time: 86.2 us -> 81.4 us (0.944)
  Pallas kernels: 83.7 us -> 79.1 us
    pallas_call x1, Pallas kernels: 81.3 us -> 76.7 us  [shards(): pl.pallas_call(kernel, out_shape=(jax.ShapeDtypeStruct((T, C), BF16), jax...]
where the time goes in v5:
time: 81.4 us; the launch traced here: 79.9 us
  Pallas kernels  79.1 us (97%)
  between operations  0.82 us (1%)
    pallas_call x1, Pallas kernels, shards(): pl.pallas_call(kernel, out_shape=(jax.ShapeDtypeStruct((T, C), BF16), jax...  76.7 us
    pallas_call x1, Pallas kernels, hand_out(): pl.pallas_call(hand_out_kernel, out_shape=tuple((jax.ShapeDtypeStruct(a.s...  2.36 us

profile of v5, /device:TPU:2, one launch (start us, length us, event | category | flops | bytes accessed | tf_op | source)
XLA Modules:
  0.0 79.9 jit_solution(16415477708754160812)
XLA Ops:
  0.6 76.7 %routed_attention.1 = (bf16[256,512]{1,0:T(8,128)(2,1)}, bf16[256,1024]{1,0:T(8,128)(2,1)}, f32[2,256,512]{2,1,0:T(8,128)}) custom-call(bf16[1,256,4096]{2,1,0:T(8,128)(2,1)} %act.1, s32[1,256]{1,0:T(1,128)} %mod.1, bf16[1,256,512]{2,1,0:T(8,128)(2,1)} %qin.1, bf16[1,256,512]{2,1,0:T(8,128)(2,1)} %kin.1, bf16[2,256,512]{2,1,0:T(8,128)(2,1)} %win.1, ...), custom_call_target="tpu_custom_call" | custom-call | tf_op jit(solution)/shard_map/routed_attention/pallas_call | solution.py:590
  77.4 2.4 %hand_out.1 = (bf16[1,256,512]{2,1,0:T(8,128)(2,1)}, bf16[1,256,1024]{2,1,0:T(8,128)(2,1)}, f32[2,256,512]{2,1,0:T(8,128)}) custom-call(bf16[1,256,512]{2,1,0:T(8,128)(2,1)} %bitcast.3, bf16[1,256,1024]{2,1,0:T(8,128)(2,1)} %bitcast.2, f32[2,256,512]{2,1,0:T(8,128)} %get-tuple-element.8.refs_2_), custom_call_target="tpu_custom_call" | custom-call | tf_op jit(solution)/shard_map/hand_out/pallas_call | solution.py:639

commit v6 on v5

--- a/solution.py
+++ b/solution.py
@@ -242,7 +242,7 @@
                     st[u, 0, p, 4 + 2 * n + m:5 + 2 * n + m] = total[:, m * BLOCK:(m + 1) * BLOCK]
             return 0
 
-        lax.fori_loop(first, last, block, 0)
+        lax.fori_loop(first, last, block, 0, unroll=True)
 
     st_x = [[], []]
 

time: 81.4 us -> 81.4 us (level)
  no operation moved by 1% of the time
where the time goes in v6:
time: 81.4 us; the launch traced here: 79.8 us
  Pallas kernels  79 us (97%)
    pallas_call x1, Pallas kernels, shards(): pl.pallas_call(kernel, out_shape=(jax.ShapeDtypeStruct((T, C), BF16), jax...  76.7 us
    pallas_call x1, Pallas kernels, hand_out(): pl.pallas_call(hand_out_kernel, out_shape=tuple((jax.ShapeDtypeStruct(a.s...  2.36 us

profile of v6, /device:TPU:2, one launch (start us, length us, event | category | flops | bytes accessed | tf_op | source)
XLA Modules:
  0.0 79.8 jit_solution(1404773964871445808)
XLA Ops:
  0.6 76.7 %routed_attention.1 = (bf16[256,512]{1,0:T(8,128)(2,1)}, bf16[256,1024]{1,0:T(8,128)(2,1)}, f32[2,256,512]{2,1,0:T(8,128)}) custom-call(bf16[1,256,4096]{2,1,0:T(8,128)(2,1)} %act.1, s32[1,256]{1,0:T(1,128)} %mod.1, bf16[1,256,512]{2,1,0:T(8,128)(2,1)} %qin.1, bf16[1,256,512]{2,1,0:T(8,128)(2,1)} %kin.1, bf16[2,256,512]{2,1,0:T(8,128)(2,1)} %win.1, ...), custom_call_target="tpu_custom_call" | custom-call | tf_op jit(solution)/shard_map/routed_attention/pallas_call | solution.py:590
  77.3 2.4 %hand_out.1 = (bf16[1,256,512]{2,1,0:T(8,128)(2,1)}, bf16[1,256,1024]{2,1,0:T(8,128)(2,1)}, f32[2,256,512]{2,1,0:T(8,128)}) custom-call(bf16[1,256,512]{2,1,0:T(8,128)(2,1)} %bitcast.3, bf16[1,256,1024]{2,1,0:T(8,128)(2,1)} %bitcast.2, f32[2,256,512]{2,1,0:T(8,128)} %get-tuple-element.8.refs_2_), custom_call_target="tpu_custom_call" | custom-call | tf_op jit(solution)/shard_map/hand_out/pallas_call | solution.py:639
